TPU v7x, 128 devices: a whole 4x4x4 slice. The times are simulated.
128 devices in a mesh: clip: 8 (over x, y_lo), fsdp: 16 (over y_hi, z, core).
Axes of the slice: x: 4, y: 4 (y_hi: 2, y_lo: 2; y = y_hi * 2 + y_lo), z: 4, core: 2. Of those that a mesh axis runs over, the one named last changes fastest.
Arguments:
- sample: bfloat16 [16384, 5120], P('clip', 'fsdp'), may hold values from -150 to 150
- noise: bfloat16 [16384, 5120], P('clip', 'fsdp'), may hold values from -6 to 6
- gen_branch: bfloat16 [16384, 5120], P('clip', 'fsdp'), may hold values from -6 to 6
- step: int32 [8], P('clip'), may hold values from 20 to 979
- teacher_mod: float32 [8, 2, 5120], P('clip'), may hold values from -3 to 3
- fake_mod: float32 [8, 2, 5120], P('clip'), may hold values from -3 to 3
- teacher_weight: bfloat16 [5120, 5120], P('clip', 'fsdp'), may hold values from -0.078125 to 0.078125
- fake_weight: bfloat16 [5120, 5120], P('clip', 'fsdp'), may hold values from -0.078125 to 0.078125
- gen_gate: float32 [8, 5120], P('clip', 'fsdp'), may hold values from -4 to 4
Outputs:
- branch_cot: bfloat16 [16384, 5120], P('clip', 'fsdp')
- gate_grad: float32 [8, 5120], P('clip', 'fsdp')
- fake_grad: float32 [5120, 5120], P('clip', 'fsdp')
All inputs are finite; a program needn't handle non-finite values. Where the computation divides by a largest or mean magnitude, that divisor is 1e-20 or more.
Results may differ from a plain program's by a relative error of at most 0.017.
Values may be sent and summed in bfloat16 or wider, within the bound.
A program may use at most 128 MiB of HBM per device.

v0:
```python
import math

import jax
import jax.numpy as jnp
from jax import lax
from jax.sharding import PartitionSpec as P

EPS = 1e-06


def per_device(
    sample, noise, gen_branch, step, teacher_mod, fake_mod, teacher_weight, fake_weight, gen_gate
):
    clip_rows = sample.shape[0]
    width = sample.shape[1] * lax.axis_size("fsdp")
    total_tokens = clip_rows * lax.axis_size("clip")
    frac = step.astype(jnp.float32)[0] / 1000.0
    sigma = 5.0 * frac / (1.0 + 4.0 * frac)
    sample32 = sample.astype(jnp.float32)
    noise32 = noise.astype(jnp.float32)
    noised = ((1.0 - sigma) * sample32 + sigma * noise32).astype(jnp.bfloat16)
    noised32 = noised.astype(jnp.float32)
    partial_sum = jnp.sum(noised32, axis=1)
    partial_power = jnp.sum(noised32 * noised32, axis=1)
    row_sum, row_total = lax.psum((partial_sum, partial_power), "fsdp")
    center = row_sum / width
    variance = jnp.maximum(row_total / width - center * center, 0.0)
    row_factor = lax.rsqrt(variance + EPS)
    local_normed = ((noised32 - center[:, None]) * row_factor[:, None]).astype(jnp.bfloat16)
    normed = lax.all_gather(local_normed, "fsdp", axis=1, tiled=True)
    normed32 = normed.astype(jnp.float32)
    teacher_in = (normed32 * (1.0 + teacher_mod[0, 1]) + teacher_mod[0, 0]).astype(jnp.bfloat16)
    fake_in = (normed32 * (1.0 + fake_mod[0, 1]) + fake_mod[0, 0]).astype(jnp.bfloat16)
    left_fake = fake_in
    teacher_velocity = jnp.dot(
        teacher_in,
        lax.all_gather(teacher_weight, "clip", axis=0, tiled=True),
        preferred_element_type=jnp.float32,
    )
    fake_velocity = jnp.dot(
        left_fake,
        lax.all_gather(fake_weight, "clip", axis=0, tiled=True),
        preferred_element_type=jnp.float32,
    )
    target = noise32 - sample32
    teacher_estimate = noised32 - sigma * teacher_velocity
    fake_estimate = noised32 - sigma * fake_velocity
    local_gap = jnp.sum(jnp.abs(sample32 - teacher_estimate))
    gap_value = lax.psum(local_gap, "fsdp") / (clip_rows * width)
    push = (fake_estimate - teacher_estimate) / (gap_value + EPS)
    branch_cot = (gen_gate * push).astype(jnp.bfloat16)
    gate_grad = jnp.sum(push * gen_branch.astype(jnp.float32), axis=0, keepdims=True) / math.sqrt(
        clip_rows
    )
    velocity_error = ((fake_velocity - target) / math.sqrt(total_tokens)).astype(jnp.bfloat16)
    left_fake = fake_in
    fake_grad = lax.psum_scatter(
        lax.dot_general(
            left_fake, velocity_error, (((0,), (0,)), ((), ())), preferred_element_type=jnp.float32
        ).astype(jnp.bfloat16),
        "clip",
        scatter_dimension=0,
        tiled=True,
    ).astype(jnp.float32)
    return (branch_cot, gate_grad, fake_grad)


def solution(mesh):
    placed = (
        P("clip", "fsdp"),
        P("clip", "fsdp"),
        P("clip", "fsdp"),
        P("clip"),
        P("clip", None, None),
        P("clip", None, None),
        P("clip", "fsdp"),
        P("clip", "fsdp"),
        P("clip", "fsdp"),
    )
    return jax.shard_map(
        per_device,
        mesh=mesh,
        in_specs=placed,
        out_specs=(P("clip", "fsdp"), P("clip", "fsdp"), P("clip", "fsdp")),
        check_vma=False,
    )
```

profile of v0, /device:TPU:1, one launch (start us, length us, event | category | flops | bytes accessed | tf_op | source)
XLA Modules:
  0.0 427.1 jit_solution(342703539540208785)
XLA Ops:
  7.2 0.0 all-gather.8.cloned.1.call-start
  7.2 0.7 all-gather.8.cloned.1.call-update
  7.9 0.0 all-gather.4.cloned.1.call-start
  8.6 2.5 convert_reduce_fusion
  11.1 0.0 copy-start.3
  11.1 0.0 copy-start.4
  11.1 0.0 copy-start.5
  11.1 0.0 copy-start
  11.1 72.0 %all-reduce = (f32[2048]{0:T(1024)S(1)}, f32[2048]{0:T(1024)S(1)}) all-reduce(f32[2048]{0:T(1024)S(1)} %get-tuple-element.4, f32[2048]{0:T(1024)S(1)} %get-tuple-element.3), channel_id=1, replica_groups=mesh['clip'=8,'fsdp'=16] {'fsdp'}, use_global_device_ids=true, to_apply=%region_3.0 | all-reduce | flops 4096 | bytes 32768 | tf_op jit(solution)/shard_map/psum | solution.py:25
  83.2 1.4 fusion.21
  84.6 0.0 all-gather.4.cloned.1.call-update
  84.6 0.0 all-gather.6.cloned.1.call-start
  84.7 0.7 all-gather.6.cloned.1.call-update
  85.4 0.0 reduce-scatter.4.cloned.1.call-start
  85.4 0.0 copy-done.3
  85.5 0.0 copy-done.4
  85.5 0.0 copy-done.5
  85.6 0.5 all-gather.8.cloned.1.call-done
  86.0 139.7 %all-gather.4.cloned.1.call-done = bf16[2048,5120]{0,1:T(8,128)(2,1)} async-done(((bf16[2048,320]{0,1:T(8,128)(2,1)}), bf16[2048,5120]{0,1:T(8,128)(2,1)}) %all-gather.4.cloned.1.call-update) | async-done | bytes 20971536 | tf_op jit(solution)/shard_map/all_gather | solution.py:30
  225.7 17.5 %fusion.16 = (f32[]{:T(128)}, f32[2048,320]{0,1:T(8,128)}) fusion(bf16[2048,320]{0,1:T(8,128)(2,1)S(1)} %copy-done, bf16[5120,320]{0,1:T(8,128)(2,1)} %all-gather.8.cloned.1.call-done, bf16[2048,5120]{0,1:T(8,128)(2,1)} %all-gather.4.cloned.1.call-done, f32[5120]{0:T(1024)S(1)} %bitcast.13, f32[5120]{0:T(1024)S(1)} %bitcast.12, f32[]{:T(128)} %bitcast, ...), kind=kOutput, calls=%fused_computation.23 | convolution fusion | flops 6757416960 | bytes 29532168 | tf_op jit(solution)/shard_map/dot_general | solution.py:35
  243.2 35.7 %psum.23 = f32[]{:T(128)} all-reduce(f32[]{:T(128)} %get-tuple-element.16), channel_id=1, replica_groups=mesh['clip'=8,'fsdp'=16] {'fsdp'}, use_global_device_ids=true, to_apply=%region_5.0 | all-reduce | flops 1 | bytes 8 | tf_op jit(solution)/shard_map/psum | solution.py:49
  279.6 0.0 copy-start.6
  279.6 19.1 %fusion.1 = bf16[2048,5120]{0,1:T(8,128)(2,1)} fusion(bf16[2048,5120]{0,1:T(8,128)(2,1)} %all-gather.4.cloned.1.call-done, f32[5120]{0:T(1024)S(1)} %bitcast.11, f32[5120]{0:T(1024)S(1)} %bitcast.10), kind=kLoop, calls=%fused_computation.3 | loop fusion | flops 41943040 | bytes 41984000 | tf_op jit(solution)/shard_map/convert_element_type | solution.py:33
  298.7 0.0 copy-start.2
  298.7 14.0 %multiply_reduce_fusion = (f32[320]{0:T(512)S(1)}, bf16[2048,320]{0,1:T(8,128)(2,1)}, f32[2048,320]{0,1:T(8,128)S(1)}) fusion(bf16[2048,320]{0,1:T(8,128)(2,1)S(1)} %copy-done.6, f32[]{:T(128)S(6)} %add.78, f32[2048,320]{0,1:T(8,128)} %get-tuple-element.17, f32[]{:T(128)} %bitcast, bf16[2048,320]{0,1:T(8,128)(2,1)S(1)} %get-tuple-element.7, ...), kind=kOutput, calls=%fused_computation.32 | convolution fusion | flops 6717439488 | bytes 33425928 | tf_op jit(solution)/shard_map/dot_general | solution.py:40
  312.7 11.3 %convolution_convert_fusion = bf16[5120,320]{0,1:T(8,128)(2,1)S(1)} fusion(bf16[2048,5120]{0,1:T(8,128)(2,1)} %fusion.1, f32[2048,320]{0,1:T(8,128)S(1)} %get-tuple-element.18, bf16[2048,320]{0,1:T(8,128)(2,1)S(1)} %copy-done.1, bf16[2048,320]{0,1:T(8,128)(2,1)S(1)} %copy-done.2), kind=kOutput, calls=%fused_computation.9 | convolution fusion | flops 6716456960 | bytes 29491200 | tf_op jit(solution)/shard_map/dot_general | solution.py:58
  324.0 3.6 copy.12
  327.6 0.0 reduce-scatter.4.cloned.1.call-update
  327.7 0.6 div.45
  328.2 90.1 %reduce-scatter.4.cloned.1.call-done = bf16[640,320]{1,0:T(8,128)(2,1)} async-done(((bf16[5120,320]{1,0:T(8,128)(2,1)}), bf16[640,320]{1,0:T(8,128)(2,1)}) %reduce-scatter.4.cloned.1.call-update) | async-done | bytes 409616
  418.3 1.3 copy.13
  419.6 0.9 convert_element_type.55
  (11 shorter events, 0.1 us)
Async XLA Ops:
  7.2 78.9 %all-gather.8.cloned.1.call-start = ((), (), s32[]{:S(2)}) async-start(), calls=%async_computation.3 | async-start | bytes 3686400 | tf_op jit(solution)/shard_map/all_gather | solution.py:37
  7.9 217.8 %all-gather.4.cloned.1.call-start = ((), (), s32[]{:S(2)}) async-start(), calls=%async_computation.1 | async-start | bytes 22282240 | tf_op jit(solution)/shard_map/all_gather | solution.py:30
  11.1 74.3 %copy-start.3 = (f32[1,2,5120]{2,1,0:T(2,128)S(1)}, f32[1,2,5120]{2,1,0:T(2,128)}, u32[]{:S(2)}) copy-start(f32[1,2,5120]{2,1,0:T(2,128)} %param.14) | copy-start | bytes 122884
  11.1 74.4 %copy-start.4 = (f32[1,2,5120]{2,1,0:T(2,128)S(1)}, f32[1,2,5120]{2,1,0:T(2,128)}, u32[]{:S(2)}) copy-start(f32[1,2,5120]{2,1,0:T(2,128)} %param.13) | copy-start | bytes 122884
  11.1 74.4 %copy-start.5 = (f32[1,320]{1,0:T(1,128)S(1)}, f32[1,320]{1,0:T(1,128)}, u32[]{:S(2)}) copy-start(f32[1,320]{1,0:T(1,128)} %param.17) | copy-start | bytes 3844
  11.1 214.6 %copy-start = (bf16[2048,320]{0,1:T(8,128)(2,1)S(1)}, bf16[2048,320]{0,1:T(8,128)(2,1)}, u32[]{:S(2)}) copy-start(bf16[2048,320]{0,1:T(8,128)(2,1)} %param.9) | copy-start | bytes 3932164
  84.6 214.1 %all-gather.6.cloned.1.call-start = ((), (), s32[]{:S(2)}) async-start(), calls=%async_computation.2 | async-start | bytes 3686400 | tf_op jit(solution)/shard_map/all_gather | solution.py:42
  85.4 333.0 %reduce-scatter.4.cloned.1.call-start = ((), (), s32[]{:S(2)}) async-start(), calls=%async_computation.4 | async-start | bytes 4423680
  279.6 19.1 %copy-start.6 = (bf16[2048,320]{0,1:T(8,128)(2,1)S(1)}, bf16[2048,320]{0,1:T(8,128)(2,1)}, u32[]{:S(2)}) copy-start(bf16[2048,320]{0,1:T(8,128)(2,1)} %param.11) | copy-start | bytes 3932164
  298.7 14.0 %copy-start.1 = (bf16[2048,320]{0,1:T(8,128)(2,1)S(1)}, bf16[2048,320]{0,1:T(8,128)(2,1)}, u32[]{:S(2)}) copy-start(bf16[2048,320]{0,1:T(8,128)(2,1)} %param.9) | copy-start | bytes 3932164
  298.7 14.0 %copy-start.2 = (bf16[2048,320]{0,1:T(8,128)(2,1)S(1)}, bf16[2048,320]{0,1:T(8,128)(2,1)}, u32[]{:S(2)}) copy-start(bf16[2048,320]{0,1:T(8,128)(2,1)} %param.10) | copy-start | bytes 3932164
Sparse Core Ops, SparseCore 0:
  9.7 76.3 all-gather.7
  89.1 136.6 all-gather.3
  227.4 69.8 all-gather.5
  327.8 90.5 reduce-scatter.3
where the time goes:
time: 427 us
  waiting for transfers between devices  232 us (54%)
  blocking collectives  108 us (25%)
  matrix products  42.8 us (10%)
  other arithmetic  24 us (6%)
  between operations  15.2 us (4%)
  local copies, waits for them, and re-layouts  5.49 us (1%)
    all_gather x1, waiting for transfers between devices, per_device(): normed = lax.all_gather(local_normed, 'fsdp', axis=1, tiled=True)  140 us
    unnamed x5, waiting for transfers between devices  91.5 us
    psum x1, blocking collectives, per_device(): row_sum, row_total = lax.psum((partial_sum, partial_power), 'fsdp')  72 us
    psum x1, blocking collectives, per_device(): gap_value = lax.psum(local_gap, 'fsdp') / (clip_rows * width)  35.7 us
    convert_element_type x1, other arithmetic, per_device(): (normed32 * (1.0 + fake_mod[0, 1]) + fake_mod[0, 0]).astype(jnp.bfloat16)  19.1 us
    dot_general x1, matrix products, per_device(): jnp.dot(teacher_in, lax.all_gather(teacher_weight, 'clip', axis=0, tiled=...  17.5 us
    dot_general x1, matrix products, per_device(): jnp.dot(left_fake, lax.all_gather(fake_weight, 'clip', axis=0, tiled=True...  14 us
    dot_general x1, matrix products, per_device(): lax.dot_general(left_fake, velocity_error, (((0,), (0,)), ((), ())), pref...  11.3 us
  transfers between devices with their start and end apart: 4, of which 3 were waited for; matrix products, arithmetic and copies ran while one was open for 10% of the time, Pallas kernels for 0%

commit v1 on v0

v1 whole, which is shorter than its diff:
```python
import functools
import math

import jax
import jax.numpy as jnp
from jax import lax
from jax.experimental import pallas as pl
from jax.experimental.pallas import tpu as pltpu
from jax.sharding import PartitionSpec as P

EPS = 1e-06
F32 = jnp.float32
BF16 = jnp.bfloat16
NT = (((1,), (1,)), ((), ()))

TOK = 2048
FB = 320
CB = 640
CLIPS = 8
COPIES = 64


def eye(n, dtype):
    same = lax.broadcasted_iota(jnp.int32, (n, n), 0) == lax.broadcasted_iota(jnp.int32, (n, n), 1)
    return same.astype(F32).astype(dtype)


def transposed(x):
    return lax.dot_general(eye(x.shape[1], BF16), x, NT, preferred_element_type=F32)


def kernel(
    sample, noise, gen, step, tmod, fmod, tw, fw, gate,
    bc_out, gg_out, fg_out,
    at, wt, acc, xs, ws, sT, nT, gT, vv, st1, st2, piv, mr, cs, bw, sv, sb, col,
    gopp, gnb, gy, gown, ropp, rnb, ry, fg, gap_s, gap_r,
    send_sems, recv_sems, loc_sems,
):
    clip = lax.axis_index("clip")
    fs = lax.axis_index("fsdp")
    x, l = clip // 2, clip % 2
    p, z, yh = fs % 2, (fs // 2) % 4, fs // 8
    s = 1 - 2 * p
    zu, zd, zo = (z + s + 4) % 4, (z - s + 4) % 4, (z + 2) % 4
    yo = 1 - yh
    xr, xl, xo = (x + 1) % 4, (x + 3) % 4, (x + 2) % 4

    def q(y, zz):
        return y * 4 + zz

    def on_f(y, zz, pp):
        return {"fsdp": (y * 4 + zz) * 2 + pp}

    def on_c(xx, ll):
        return {"clip": xx * 2 + ll}

    up, dn, across, sib = on_f(yh, zu, p), on_f(yh, zd, p), on_f(yo, z, p), on_f(yh, z, 1 - p)
    right, left, pair = on_c(xr, l), on_c(xl, l), on_c(x, 1 - l)
    me, u, d, o = q(yh, z), q(yh, zu), q(yh, zd), q(yh, zo)
    y_me, y_u, y_d, y_o = q(yo, z), q(yo, zu), q(yo, zd), q(yo, zo)

    table = {}

    def copy(name, src, dst, to):
        i = len(table)
        assert i < COPIES
        c = pltpu.make_async_remote_copy(
            src_ref=src, dst_ref=dst, send_sem=send_sems.at[i], recv_sem=recv_sems.at[i],
            device_id=to, device_id_type=pl.DeviceIdType.MESH,
        )
        table[name] = [c, False]
        c.start()

    def got(*names):
        for name in names:
            table[name][0].wait_recv()

    def sent(*names):
        for name in names:
            if not table[name][1]:
                table[name][1] = True
                table[name][0].wait_send()

    part = {
        "a": (pl.multiple_of(p * 512, 128), 128),
        "b": (pl.multiple_of(128 + p * 256, 128), 128),
        "c": (pl.multiple_of(256 + p * 64, 64), 64),
        "ab": (pl.multiple_of(p * 384, 128), 256),
        "all": (pl.multiple_of(p * 320, 64), 320),
    }

    def send(name, block, which, to):
        ref = at.at[block, pl.ds(*part[which]), :]
        copy(name, ref, ref, to)

    def send_w(name, block, half, to):
        ref = wt.at[block, pl.ds(half * FB, FB), :]
        copy(name, ref, ref, to)

    loads = []
    for i, (src, dst) in enumerate(
        [(sample, xs.at[0]), (noise, xs.at[1]), (fw, ws.at[0]), (tw, ws.at[1]), (gen, xs.at[2])]
    ):
        loads.append(pltpu.make_async_copy(src, dst, loc_sems.at[i]))
        loads[-1].start()
    barrier = pltpu.get_barrier_semaphore()
    for to in (up, dn, across, sib, right, left, pair):
        pl.semaphore_signal(barrier, inc=1, device_id=to, device_id_type=pl.DeviceIdType.MESH)

    frac = jnp.full((8, 128), step[0], jnp.int32).astype(F32) / 1000.0
    sigma = (5.0 * frac / (1.0 + 4.0 * frac))[0:1, 0:1]

    loads[0].wait()
    loads[1].wait()

    @pl.loop(0, 8)
    def _(i):
        rows = pl.ds(pl.multiple_of(i * 256, 256), 256)
        s32 = xs[0, rows, :].astype(F32)
        n32 = xs[1, rows, :].astype(F32)
        noised = ((1.0 - sigma) * s32 + sigma * n32).astype(BF16)
        at[me, pl.ds(*part["all"]), rows] = transposed(noised).astype(BF16)

    pl.semaphore_wait(barrier, 7)
    send("up_a", me, "a", up)
    send("dn_b", me, "b", dn)
    send("up_c", me, "c", up)
    send("dn_a", me, "a", dn)
    send("y_own", me, "all", across)
    send("s_own", me, "all", sib)

    loads[2].wait()
    wt[clip, 0:FB, :] = transposed_w(ws, 0)
    send_w("xr_f", clip, 0, right)
    send_w("pair_f", clip, 0, pair)
    loads[3].wait()
    wt[clip, FB:CB, :] = transposed_w(ws, 1)
    send_w("xl_t", clip, 1, left)
    send_w("xr_t", clip, 1, right)
    send_w("xl_f", clip, 0, left)
    send_w("pair_t", clip, 1, pair)

    w_l, w_r, w_o = xl * 2 + l, xr * 2 + l, xo * 2 + l
    v_me, v_l, v_r, v_o = x * 2 + 1 - l, xl * 2 + 1 - l, xr * 2 + 1 - l, xo * 2 + 1 - l

    loads[4].wait()

    @pl.loop(0, 8)
    def _(i):
        rows = pl.ds(pl.multiple_of(i * 256, 256), 256)
        sT[:, rows] = transposed(xs[0, rows, :]).astype(BF16)
        nT[:, rows] = transposed(xs[1, rows, :]).astype(BF16)
        gT[:, rows] = transposed(xs[2, rows, :]).astype(BF16)
        own = at[me, pl.ds(*part["all"]), rows].astype(F32)
        piv[:, rows] = jnp.sum(own, axis=0, keepdims=True) * (1.0 / FB)
        st1[:, rows] = jnp.zeros((8, 256), F32)
        st2[:, rows] = jnp.zeros((8, 256), F32)
        acc[:, rows] = jnp.zeros((CB, 256), F32)

    cs[...] = jnp.zeros_like(cs)
    bw[...] = jnp.zeros_like(bw)
    sv[...] = jnp.zeros_like(sv)
    sb[...] = jnp.zeros_like(sb)

    def stats(block, first, rows):
        @pl.loop(0, 8)
        def _(i):
            cols = pl.ds(pl.multiple_of(i * 256, 256), 256)
            v = at[block, first : first + rows, cols].astype(F32) - piv[:, cols]
            v = v.reshape(rows // 8, 8, 256)
            st1[:, cols] += jnp.sum(v, axis=0)
            st2[:, cols] += jnp.sum(v * v, axis=0)

    def scale(block):
        for h, mod in ((0, fmod), (1, tmod)):
            lanes = pl.ds(pl.multiple_of(block * CB, 128), CB)
            factor = 1.0 + mod[1:2, lanes]
            shift = mod[0:1, lanes]

            @pl.loop(0, 5)
            def _(i):
                rows = pl.ds(pl.multiple_of(h * FB + i * 64, 64), 64)
                w = wt[block, rows, :].astype(F32)
                scaled = (w * factor).astype(BF16)
                wt[block, rows, :] = scaled
                back, moved = scaled.astype(F32), w * shift
                cs[rows, :] += sum(back[:, k : k + 128] for k in range(0, CB, 128))
                bw[rows, :] += sum(moved[:, k : k + 128] for k in range(0, CB, 128))

    def forward(block, first, rows, top=0, n=CB):
        @pl.loop(0, 4)
        def _(i):
            cols = pl.ds(pl.multiple_of(i * 512, 512), 512)
            acc[top : top + n, cols] += jnp.dot(
                wt[block, top : top + n, first : first + rows],
                at[block, first : first + rows, cols],
                preferred_element_type=F32,
            )

    got("xr_f")
    send_w("xr_of", w_l, 0, right)
    got("xl_t")
    send_w("xl_ot", w_r, 1, left)
    got("up_a")
    send("up_oa", d, "a", up)
    got("dn_b")
    send("dn_ob", u, "b", dn)
    send("dn_c", me, "c", dn)
    got("up_c")
    send("up_oc", d, "c", up)
    send("up_b", me, "b", up)
    got("pair_f")
    send_w("xr_vf", v_me, 0, right)
    got("pair_t")
    send_w("xl_vt", v_me, 1, left)
    send_w("xr_vt", v_me, 1, right)
    send_w("xl_vf", v_me, 0, left)
    got("s_own")
    stats(me, 0, CB)
    got("up_oa")
    send("y_oa", o, "a", across)
    got("y_own")
    send("up_yab", y_me, "ab", up)
    send("dn_yab", y_me, "ab", dn)
    send("up_yc", y_me, "c", up)
    send("dn_yc", y_me, "c", dn)
    send("s_y", y_me, "all", sib)
    got("dn_ob")
    send("y_ob", o, "b", across)
    got("up_oc")
    send("y_oc", o, "c", across)
    send("s_o", o, "all", sib)
    got("xr_t", "xl_f", "xr_of", "xl_ot")
    sent("xr_f", "xr_t", "xl_f", "xl_t", "pair_f", "pair_t", "xr_of", "xl_ot")
    for block in (clip, w_l, w_r, w_o):
        scale(block)
    got("xr_vf")
    send_w("xr_vof", v_l, 0, right)
    got("xl_vt")
    send_w("xl_vot", v_r, 1, left)
    got("s_y")
    stats(y_me, 0, CB)
    got("s_o")
    stats(o, 0, CB)
    got("dn_a", "dn_c")
    send("s_u", u, "all", sib)
    got("up_b")
    send("s_d", d, "all", sib)
    got("s_d")
    stats(u, 0, CB)
    got("s_u")
    stats(d, 0, CB)
    got("xr_vt", "xl_vf", "xr_vof", "xl_vot")
    sent("xr_vf", "xr_vt", "xl_vf", "xl_vt", "xr_vof", "xl_vot")
    for block in (v_me, v_l, v_r, v_o):
        scale(block)
    cs[...] = jnp.broadcast_to(jnp.sum(cs[...], axis=1, keepdims=True), cs.shape)
    bw[...] = jnp.broadcast_to(jnp.sum(bw[...], axis=1, keepdims=True), bw.shape)
    for block in (me, u, d, o, y_me):
        forward(block, 0, CB)
    got("y_oa", "y_ob", "y_oc")
    send("s_yo", y_o, "all", sib)
    got("dn_yab")
    send("s_yu", y_u, "ab", sib)
    got("up_yab")
    send("s_yd", y_d, "ab", sib)
    got("s_yo")
    stats(y_o, 0, CB)
    forward(y_o, 0, CB)
    got("s_yd", "s_yu")
    for block in (y_u, y_d):
        for first in (0, 384):
            stats(block, first, 256)
            forward(block, first, 256)
    got("dn_yc")
    send("s_yuc", y_u, "c", sib)
    got("up_yc")
    send("s_ydc", y_d, "c", sib)
    got("s_yuc", "s_ydc")
    for block in (y_u, y_d):
        stats(block, 256, 128)
        forward(block, 256, 128, 0, FB)

    shift = jnp.sum(st1[...], axis=0, keepdims=True) * (1.0 / (CLIPS * CB))
    power = jnp.sum(st2[...], axis=0, keepdims=True) * (1.0 / (CLIPS * CB))
    mr[0:1, :] = piv[...] + shift
    mr[1:2, :] = lax.rsqrt(jnp.maximum(power - shift * shift, 0.0) + EPS)

    @pl.loop(0, 40)
    def _(i):
        rows = pl.ds(pl.multiple_of((i // 8) * 64, 64), 64)
        cols = pl.ds(pl.multiple_of((i % 8) * 256, 256), 256)
        m, r = mr[0:1, cols], mr[1:2, cols]
        fv = r * (acc[rows, cols] - cs[rows, 0:1] * m) + bw[rows, 0:1]
        acc[rows, cols] = fv
        target = nT[rows, cols].astype(F32) - sT[rows, cols].astype(F32)
        err = (fv - target) * (1.0 / math.sqrt(CLIPS * TOK))
        v = (r * err).astype(BF16)
        vv[rows, cols] = v
        mv = m * v.astype(F32)
        sv[rows, :] += mv[:, :128] + mv[:, 128:]
        sb[rows, :] += err[:, :128] + err[:, 128:]

    sv[...] = jnp.broadcast_to(jnp.sum(sv[...], axis=1, keepdims=True), sv.shape)
    sb[...] = jnp.broadcast_to(jnp.sum(sb[...], axis=1, keepdims=True), sb.shape)

    def grad(block, dst):
        for first, n in ((0, 256), (256, 256), (512, 128)):
            lanes = pl.ds(pl.multiple_of(block * CB + first, 128), n)
            part_sum = lax.dot_general(
                vv[...], at[block, first : first + n, :], NT, preferred_element_type=F32
            )
            g = (part_sum - sv[:, 0:1]) * (1.0 + fmod[1:2, lanes]) + sb[:, 0:1] * fmod[0:1, lanes]
            dst[:, first : first + n] = g.astype(dst.dtype)

    HALF = FB // 2
    lo, hi = slice(0, HALF), slice(HALF, FB)
    ls = (1 - l, l)
    for j in (0, 1):
        grad(xo * 2 + ls[j], gopp.at[j])
        copy(f"or{j}", gopp.at[j, lo], ropp.at[0, j], right)
        copy(f"ol{j}", gopp.at[j, hi], ropp.at[1, j], left)
    for j in (0, 1):
        grad(xr * 2 + ls[j], gnb.at[0, j])
        copy(f"rr{j}", gnb.at[0, j, hi], rnb.at[0, j, hi], right)
        grad(xl * 2 + ls[j], gnb.at[1, j])
        copy(f"rl{j}", gnb.at[1, j, lo], rnb.at[1, j, lo], left)
        got(f"or{j}")
        gnb[0, j, lo] = (gnb[0, j, lo].astype(F32) + ropp[0, j].astype(F32)).astype(BF16)
        copy(f"sr{j}", gnb.at[0, j, lo], rnb.at[0, j, lo], right)
        got(f"ol{j}")
        gnb[1, j, hi] = (gnb[1, j, hi].astype(F32) + ropp[1, j].astype(F32)).astype(BF16)
        copy(f"sl{j}", gnb.at[1, j, hi], rnb.at[1, j, hi], left)
    for j in (0, 1):
        grad(x * 2 + ls[j], gown.at[j])

    for block in (y_u, y_d):
        forward(block, 256, 128, FB, FB)

    col[...] = jnp.zeros_like(col)

    @pl.loop(0, 40)
    def _(i):
        rows = pl.ds(pl.multiple_of((i // 8) * 64, 64), 64)
        more = pl.ds(pl.multiple_of(FB + (i // 8) * 64, 64), 64)
        own = pl.ds(pl.multiple_of(p * FB + (i // 8) * 64, 64), 64)
        cols = pl.ds(pl.multiple_of((i % 8) * 256, 256), 256)
        m, r = mr[0:1, cols], mr[1:2, cols]
        tv = r * (acc[more, cols] - cs[more, 0:1] * m) + bw[more, 0:1]
        diff = sigma * (tv - acc[rows, cols])
        acc[more, cols] = diff
        away = jnp.abs(
            sT[rows, cols].astype(F32) - (at[me, own, cols].astype(F32) - sigma * tv)
        )
        pushed = diff * gT[rows, cols].astype(F32)
        col[0, rows, :] += away[:, :128] + away[:, 128:]
        col[1, rows, :] += pushed[:, :128] + pushed[:, 128:]

    total = jnp.sum(jnp.sum(col[0], axis=0, keepdims=True), axis=1, keepdims=True)
    total = jnp.broadcast_to(total, (8, 128))
    for k, to in enumerate(
        (sib, on_f(yh, z + 1 - 2 * (z % 2), p), on_f(yh, 3 - z, p), across)
    ):
        gap_s[k] = total
        copy(f"gap{k}", gap_s.at[k], gap_r.at[k], to)
        got(f"gap{k}")
        total = total + gap_r[k]
    weight = 1.0 / (total[0:1, 0:1] * (1.0 / (TOK * CLIPS * CB)) + EPS)

    same = eye(FB, F32)
    gate_col = jnp.sum(same * gate[...], axis=1, keepdims=True) * weight
    col[0] = jnp.broadcast_to(gate_col, (FB, 128))
    gg_col = jnp.sum(col[1], axis=1, keepdims=True) * weight * (1.0 / math.sqrt(TOK))
    gg_out[...] = jnp.sum(same * gg_col, axis=0, keepdims=True)

    @pl.loop(0, 8)
    def _(i):
        rows = pl.ds(pl.multiple_of(i * 256, 256), 256)
        cot = (col[0, :, 0:1] * acc[FB:CB, rows]).astype(BF16)
        xs[0, rows, :] = lax.dot_general(
            eye(256, BF16), cot, NT, preferred_element_type=F32
        ).astype(BF16)

    out_bc = pltpu.make_async_copy(xs.at[0], bc_out, loc_sems.at[5])
    out_bc.start()

    got("rr0", "sr0", "rl0", "sl0")
    for k, rows in enumerate((lo, hi)):
        gy[rows] = (
            gown[0, rows] + rnb[0, 0, rows].astype(F32) + rnb[1, 0, rows].astype(F32)
        ).astype(BF16)
        copy(f"y{k}", gy.at[rows], ry.at[rows], pair)
    got("rr1", "sr1", "rl1", "sl1")
    gown[1] = gown[1] + rnb[0, 1].astype(F32) + rnb[1, 1].astype(F32)
    got("y0", "y1")
    for k in range(0, CB, 128):
        lanes = slice(k, k + 128)
        whole = gown[1, :, lanes] + ry[:, lanes].astype(F32)
        high = whole.astype(BF16)
        low = (whole - high.astype(F32)).astype(BF16)
        fg[lanes, :] = transposed(high) + transposed(low)
    out_fg = pltpu.make_async_copy(fg, fg_out, loc_sems.at[6])
    out_fg.start()
    sent(*table)
    out_bc.wait()
    out_fg.wait()


def transposed_w(ws, i):
    return transposed(ws[i]).astype(BF16)


def per_device(
    sample, noise, gen_branch, step, teacher_mod, fake_mod, teacher_weight, fake_weight, gen_gate
):
    hbm = pl.BlockSpec(memory_space=pl.ANY)
    vmem = pl.BlockSpec(memory_space=pltpu.VMEM)
    return pl.pallas_call(
        kernel,
        out_shape=(
            jax.ShapeDtypeStruct((TOK, FB), BF16),
            jax.ShapeDtypeStruct((1, FB), F32),
            jax.ShapeDtypeStruct((CB, FB), F32),
        ),
        in_specs=[
            hbm, hbm, hbm, pl.BlockSpec(memory_space=pltpu.SMEM), vmem, vmem, hbm, hbm, vmem,
        ],
        out_specs=(hbm, vmem, hbm),
        scratch_shapes=[
            pltpu.VMEM((CLIPS, CB, TOK), BF16),
            pltpu.VMEM((CLIPS, CB, CB), BF16),
            pltpu.VMEM((CB, TOK), F32),
            pltpu.VMEM((3, TOK, FB), BF16),
            pltpu.VMEM((2, CB, FB), BF16),
            pltpu.VMEM((FB, TOK), BF16),
            pltpu.VMEM((FB, TOK), BF16),
            pltpu.VMEM((FB, TOK), BF16),
            pltpu.VMEM((FB, TOK), BF16),
            pltpu.VMEM((8, TOK), F32),
            pltpu.VMEM((8, TOK), F32),
            pltpu.VMEM((1, TOK), F32),
            pltpu.VMEM((2, TOK), F32),
            pltpu.VMEM((CB, 128), F32),
            pltpu.VMEM((CB, 128), F32),
            pltpu.VMEM((FB, 128), F32),
            pltpu.VMEM((FB, 128), F32),
            pltpu.VMEM((2, FB, 128), F32),
            pltpu.VMEM((2, FB, CB), BF16),
            pltpu.VMEM((2, 2, FB, CB), BF16),
            pltpu.VMEM((FB, CB), BF16),
            pltpu.VMEM((2, FB, CB), F32),
            pltpu.VMEM((2, 2, FB // 2, CB), BF16),
            pltpu.VMEM((2, 2, FB, CB), BF16),
            pltpu.VMEM((FB, CB), BF16),
            pltpu.VMEM((CB, FB), F32),
            pltpu.VMEM((4, 8, 128), F32),
            pltpu.VMEM((4, 8, 128), F32),
            pltpu.SemaphoreType.DMA((COPIES,)),
            pltpu.SemaphoreType.DMA((COPIES,)),
            pltpu.SemaphoreType.DMA((8,)),
        ],
        compiler_params=pltpu.CompilerParams(
            collective_id=0, has_side_effects=True, vmem_limit_bytes=62 << 20
        ),
        name="step",
    )(
        sample, noise, gen_branch, step,
        teacher_mod.reshape(2, CLIPS * CB), fake_mod.reshape(2, CLIPS * CB),
        teacher_weight, fake_weight, gen_gate,
    )


def solution(mesh):
    placed = (
        P("clip", "fsdp"),
        P("clip", "fsdp"),
        P("clip", "fsdp"),
        P("clip"),
        P("clip", None, None),
        P("clip", None, None),
        P("clip", "fsdp"),
        P("clip", "fsdp"),
        P("clip", "fsdp"),
    )
    return jax.shard_map(
        per_device,
        mesh=mesh,
        in_specs=placed,
        out_specs=(P("clip", "fsdp"), P("clip", "fsdp"), P("clip", "fsdp")),
        check_vma=False,
    )
```

time: 427 us -> 184 us (0.43)
  waiting for transfers between devices: 232 us -> 0 us
  Pallas kernels: 0 us -> 168 us
  blocking collectives: 108 us -> 0 us
  matrix products: 42.8 us -> 0 us
  other arithmetic: 24 us -> 0 us
  between operations: 15.2 us -> 1.41 us
  local copies, waits for them, and re-layouts: 5.49 us -> 13 us
    pallas_call x0 -> x1, Pallas kernels: none -> 168 us  [per_device(): pl.pallas_call(kernel, out_shape=(jax.ShapeDtypeStruct((TOK, FB), BF16),...]
    all_gather x3 -> x0, waiting for transfers between devices: 140 us -> none  [the longest x1 140 us: per_device(): normed = lax.all_gather(local_normed, 'fsdp', axis=1, tiled=True)]
    psum x2 -> x0, blocking collectives: 108 us -> none  [the longest x1 72 us: per_device(): row_sum, row_total = lax.psum((partial_sum, partial_power), 'fsdp')]
    unnamed x5 -> x0, waiting for transfers between devices: 91.5 us -> none
    dot_general x3 -> x0, matrix products: 42.8 us -> none  [the longest x1 17.5 us: per_device(): jnp.dot(teacher_in, lax.all_gather(teacher_weight, 'clip', axis=0, tiled=...]
    convert_element_type x3 -> x0, other arithmetic: 21.4 us -> none  [the longest x1 19.1 us: per_device(): (normed32 * (1.0 + fake_mod[0, 1]) + fake_mod[0, 0]).astype(jnp.bfloat16)]
    unnamed x16, local copies, waits for them, and re-layouts: 4.93 us -> 9.22 us
  transfers between devices with their start and end apart: 4 -> 0, of which waited for: 3 -> 0; matrix products, arithmetic and copies ran while one was open for 10% -> 0% of each run, Pallas kernels for 0% -> 0%
where the time goes in v1:
time: 184 us; the launch traced here: 182 us
  Pallas kernels  168 us (91%)
  local copies, waits for them, and re-layouts  13 us (7%)
    pallas_call x1, Pallas kernels, per_device(): pl.pallas_call(kernel, out_shape=(jax.ShapeDtypeStruct((TOK, FB), BF16),...  168 us
    unnamed x16, local copies, waits for them, and re-layouts  9.22 us
    pallas_call x2, local copies, waits for them, and re-layouts, per_device(): pl.pallas_call(kernel, out_shape=(jax.ShapeDtypeStruct((TOK, FB), BF16),...  3.79 us

profile of v1, /device:TPU:1, one launch (start us, length us, event | category | flops | bytes accessed | tf_op | source)
XLA Modules:
  0.0 182.3 jit_solution(13099189977356521013)
XLA Ops:
  0.6 0.0 copy-start
  1.4 2.0 %copy.15.tw = bf16[640,320]{1,0:T(8,128)(2,1)} copy(bf16[640,320]{0,1:T(8,128)(2,1)} %param.15) | data formatting | bytes 819200 | tf_op args[6]
  3.4 2.0 %copy.16.fw = bf16[640,320]{1,0:T(8,128)(2,1)} copy(bf16[640,320]{0,1:T(8,128)(2,1)} %param.16) | data formatting | bytes 819200 | tf_op args[7]
  5.4 0.0 copy-done
  5.4 0.0 copy-start.1
  5.4 1.6 copy.12.sample
  6.9 0.0 copy-done.1
  6.9 0.0 copy-start.2
  6.9 1.6 copy.13.noise
  8.5 0.0 copy-done.2
  8.5 1.6 copy.14.gen
  10.0 167.9 %step.2 = (bf16[2048,320]{1,0:T(8,128)(2,1)}, f32[1,320]{1,0:T(1,128)}, f32[640,320]{1,0:T(8,128)}) custom-call(bf16[2048,320]{1,0:T(8,128)(2,1)} %copy.12.sample, bf16[2048,320]{1,0:T(8,128)(2,1)} %copy.13.noise, bf16[2048,320]{1,0:T(8,128)(2,1)} %copy.14.gen, s32[1]{0:T(128)S(6)} %copy.20.step, f32[2,5120]{1,0:T(2,128)} %bitcast.2, f32[2,5120]{1,0:T(2,128)} %bitcast.3, ...), custom_call_target="tpu_custom_call" | custom-call | tf_op jit(solution)/shard_map/step/pallas_call | solution.py:418
  177.9 0.0 copy-start.3
  177.9 2.6 %copy.17 = bf16[2048,320]{0,1:T(8,128)(2,1)} copy(bf16[2048,320]{1,0:T(8,128)(2,1)} %get-tuple-element.3) | data formatting | bytes 2621440 | tf_op jit(solution)/shard_map/step/pallas_call | solution.py:418
  180.5 0.0 copy-done.3
  180.5 0.0 copy-start.4
  180.5 1.2 copy.18
  181.7 0.0 copy-done.4
  181.7 0.6 copy.21
Async XLA Ops:
  0.6 4.7 %copy-start = (bf16[2048,320]{0,1:T(8,128)(2,1)S(1)}, bf16[2048,320]{0,1:T(8,128)(2,1)}, u32[]{:S(2)}) copy-start(bf16[2048,320]{0,1:T(8,128)(2,1)} %param.9) | copy-start | bytes 3932164
  5.4 1.6 copy-start.1
  6.9 1.6 copy-start.2
  177.9 2.6 %copy-start.3 = (f32[640,320]{1,0:T(8,128)S(1)}, f32[640,320]{1,0:T(8,128)}, u32[]{:S(2)}) copy-start(f32[640,320]{1,0:T(8,128)} %get-tuple-element.5) | copy-start | bytes 2457604
  180.5 1.2 copy-start.4

commit v2 on v1

v2 whole, which is shorter than its diff:
```python
import functools
import math

import jax
import jax.numpy as jnp
from jax import lax
from jax.experimental import pallas as pl
from jax.experimental.pallas import tpu as pltpu
from jax.sharding import PartitionSpec as P

EPS = 1e-06
F32 = jnp.float32
BF16 = jnp.bfloat16
NT = (((1,), (1,)), ((), ()))

TOK = 2048
FB = 320
CB = 640
CLIPS = 8
COPIES = 64


def eye(n):
    same = lax.broadcasted_iota(jnp.int32, (n, n), 0) == lax.broadcasted_iota(jnp.int32, (n, n), 1)
    return same.astype(F32)


def kernel(
    sample, noise, gen, step, tmod, fmod, tw, fw, gate,
    bc_out, gg_out, fg_out,
    at, wt, acc, sT, nT, gT, vv, bt, st1, st2, piv, mr, cs, bw, sv, sb, col,
    gopp, gnb, gy, gown, ropp, rnb, ry, gap_s, gap_r,
    send_sems, recv_sems, loc_sems,
):
    clip = lax.axis_index("clip")
    fs = lax.axis_index("fsdp")
    x, l = clip // 2, clip % 2
    p, z, yh = fs % 2, (fs // 2) % 4, fs // 8
    s = 1 - 2 * p
    zu, zd, zo = (z + s + 4) % 4, (z - s + 4) % 4, (z + 2) % 4
    yo = 1 - yh
    xr, xl, xo = (x + 1) % 4, (x + 3) % 4, (x + 2) % 4

    def on_f(y, zz, pp):
        return {"fsdp": (y * 4 + zz) * 2 + pp}

    def on_c(xx, ll):
        return {"clip": xx * 2 + ll}

    up, dn, across, sib = on_f(yh, zu, p), on_f(yh, zd, p), on_f(yo, z, p), on_f(yh, z, 1 - p)
    right, left, pair = on_c(xr, l), on_c(xl, l), on_c(x, 1 - l)
    me, y_me, o, u, d, y_o, y_u, y_d = range(8)

    def slot(block):
        rel = ((block % 4 - z) * s + 8) % 4
        r1, r2 = rel % 2, rel // 2
        yd = (block // 4 + yh) % 2
        return (1 - r1) * (yd + (2 + 2 * yd) * r2) + r1 * (3 + 3 * yd + r2)

    table = {}

    def copy(name, src, dst, to):
        i = len(table)
        assert i < COPIES
        c = pltpu.make_async_remote_copy(
            src_ref=src, dst_ref=dst, send_sem=send_sems.at[i], recv_sem=recv_sems.at[i],
            device_id=to, device_id_type=pl.DeviceIdType.MESH,
        )
        table[name] = [c, False]
        c.start()

    def got(*names):
        for name in names:
            table[name][0].wait_recv()

    def sent(*names):
        for name in names:
            if not table[name][1]:
                table[name][1] = True
                table[name][0].wait_send()

    part = {
        "a": (pl.multiple_of(p * 512, 128), 128),
        "b": (pl.multiple_of(128 + p * 256, 128), 128),
        "c": (pl.multiple_of(256 + p * 64, 64), 64),
        "ab": (pl.multiple_of(p * 384, 128), 256),
        "all": (pl.multiple_of(p * 320, 64), 320),
    }

    def span(block, which):
        first, n = part[which]
        return pl.ds(pl.multiple_of(block * CB + first, 64), n)

    def send(name, here, there, which, to):
        copy(name, at.at[span(here, which), :], at.at[span(there, which), :], to)

    def w_ref(block, half):
        lanes = pl.ds(pl.multiple_of(slot(block) * CB, 128), CB)
        return wt.at[pl.ds(half * FB, FB), lanes]

    def send_w(name, block, half, to):
        copy(name, w_ref(block, half), w_ref(block, half), to)

    loads = {}

    def load(name, src, dst):
        loads[name] = pltpu.make_async_copy(src, dst, loc_sems.at[len(loads)])
        loads[name].start()

    def local(which):
        first, n = part[which]
        return pl.ds(pl.multiple_of(first - p * FB, 64), n)

    for which in ("a", "b", "c"):
        load("s" + which, sample.at[local(which), :], sT.at[local(which), :])
        load("n" + which, noise.at[local(which), :], nT.at[local(which), :])
    load("fw", fw, w_ref(clip, 0))
    load("tw", tw, w_ref(clip, 1))
    load("gen", gen, gT)
    barrier = pltpu.get_barrier_semaphore()
    for to in (up, dn, across, sib, right, left, pair):
        pl.semaphore_signal(barrier, inc=1, device_id=to, device_id_type=pl.DeviceIdType.MESH)

    frac = jnp.full((8, 128), step[0], jnp.int32).astype(F32) / 1000.0
    sigma = (5.0 * frac / (1.0 + 4.0 * frac))[0:1, 0:1]

    def noised(which):
        loads["s" + which].wait()
        loads["n" + which].wait()
        first, n = part[which]
        own = pl.multiple_of(first - p * FB, 64)

        @pl.loop(0, n // 32)
        def _(i):
            rows = pl.ds(pl.multiple_of(own + i * 32, 32), 32)
            mixed = (1.0 - sigma) * sT[rows, :].astype(F32) + sigma * nT[rows, :].astype(F32)
            at[pl.ds(pl.multiple_of(first + i * 32, 32), 32), :] = mixed.astype(BF16)

    noised("a")
    pl.semaphore_wait(barrier, 7)
    send("up_a", me, d, "a", up)
    noised("b")
    send("dn_b", me, u, "b", dn)
    loads["fw"].wait()
    send_w("pair_f", clip, 0, pair)
    send("y_ab", me, y_me, "ab", across)
    send_w("xr_f", clip, 0, right)
    send_w("xl_f", clip, 0, left)
    noised("c")
    send("up_c", me, d, "c", up)
    send("dn_a", me, u, "a", dn)
    send("y_c", me, y_me, "c", across)
    send("s_own", me, me, "all", sib)
    loads["tw"].wait()
    send_w("xr_t", clip, 1, right)
    send_w("xl_t", clip, 1, left)
    send_w("pair_t", clip, 1, pair)

    w_l, w_r, w_o = xl * 2 + l, xr * 2 + l, xo * 2 + l
    v_me, v_l, v_r, v_o = x * 2 + 1 - l, xl * 2 + 1 - l, xr * 2 + 1 - l, xo * 2 + 1 - l
    everyone = (clip, w_l, w_r, w_o, v_me, v_l, v_r, v_o)

    @pl.loop(0, 8)
    def _(i):
        cols = pl.ds(pl.multiple_of(i * 256, 256), 256)
        own = at[pl.ds(*part["all"]), cols].astype(F32)
        piv[:, cols] = jnp.sum(own, axis=0, keepdims=True) * (1.0 / FB)
        st1[:, cols] = jnp.zeros((8, 256), F32)
        st2[:, cols] = jnp.zeros((8, 256), F32)

    cs[...] = jnp.zeros_like(cs)
    bw[...] = jnp.zeros_like(bw)
    sv[...] = jnp.zeros_like(sv)
    sb[...] = jnp.zeros_like(sb)
    col[...] = jnp.zeros_like(col)

    def add_stats(first, n, cols):
        v = at[first : first + n, cols].astype(F32) - piv[:, cols]
        v = v.reshape(n // 8, 8, 256)
        st1[:, cols] += jnp.sum(v, axis=0)
        st2[:, cols] += jnp.sum(v * v, axis=0)

    def stats(block, first, n):
        @pl.loop(0, 8)
        def _(i):
            add_stats(block * CB + first, n, pl.ds(pl.multiple_of(i * 256, 256), 256))

    def scale(block, h, mod):
        lanes = pl.ds(pl.multiple_of(block * CB, 128), CB)
        factor = 1.0 + mod[1:2, lanes]
        shift = mod[0:1, lanes]
        held = pl.ds(pl.multiple_of(slot(block) * CB, 128), CB)

        @pl.loop(0, 5)
        def _(i):
            rows = pl.ds(pl.multiple_of(h * FB + i * 64, 64), 64)
            w = wt[rows, held].astype(F32)
            scaled = (w * factor).astype(BF16)
            wt[rows, held] = scaled
            back, moved = scaled.astype(F32), w * shift
            cs[rows, :] += sum(back[:, k : k + 128] for k in range(0, CB, 128))
            bw[rows, :] += sum(moved[:, k : k + 128] for k in range(0, CB, 128))

    def scale_all(h, mod):
        for block in everyone:
            scale(block, h, mod)
        rows = slice(h * FB, h * FB + FB)
        for ref in (cs, bw):
            ref[rows] = jnp.broadcast_to(jnp.sum(ref[rows], axis=1, keepdims=True), (FB, 128))

    def product(top, spans, cols):
        left_side = [wt[top : top + FB, i : i + n] for i, n in spans]
        right_side = [at[i : i + n, cols] for i, n in spans]
        return jnp.dot(
            jnp.concatenate(left_side, axis=1) if len(spans) > 1 else left_side[0],
            jnp.concatenate(right_side, axis=0) if len(spans) > 1 else right_side[0],
            preferred_element_type=F32,
        )

    def forward(spans, fresh=False):
        @pl.loop(0, 8)
        def _(i):
            cols = pl.ds(pl.multiple_of(i * 256, 256), 256)
            if fresh:
                acc[0:FB, cols] = product(0, spans, cols)
            else:
                acc[0:FB, cols] += product(0, spans, cols)

    got("xr_f")
    send_w("xr_of", w_l, 0, right)
    got("pair_f")
    send_w("xr_vf", v_me, 0, right)
    send_w("xl_vf", v_me, 0, left)
    got("up_a")
    send("up_oa", d, o, "a", up)
    got("dn_b")
    send("dn_ob", u, o, "b", dn)
    send("dn_c", me, u, "c", dn)
    got("up_c")
    send("up_oc", d, o, "c", up)
    send("up_b", me, d, "b", up)
    got("s_own")
    stats(me, 0, CB)
    got("xl_vf")
    send_w("xl_vof", v_r, 0, left)
    got("xl_t")
    send_w("xl_ot", w_r, 1, left)
    got("y_ab")
    send("up_yab", y_me, y_d, "ab", up)
    send("dn_yab", y_me, y_u, "ab", dn)
    got("up_oa")
    send("y_oa", o, y_o, "a", across)
    got("dn_ob")
    send("y_ob", o, y_o, "b", across)
    got("up_oc")
    send("y_oc", o, y_o, "c", across)
    send("s_o", o, o, "all", sib)
    got("y_c")
    send("up_yc", y_me, y_d, "c", up)
    send("dn_yc", y_me, y_u, "c", dn)
    send("s_y", y_me, y_me, "all", sib)
    got("pair_t")
    send_w("xr_vt", v_me, 1, right)
    send_w("xl_vt", v_me, 1, left)
    got("xl_f", "xr_of", "xr_vf", "xl_vof")
    sent("xr_f", "xl_f", "pair_f", "xr_of", "xr_vf", "xl_vf", "xl_vof")
    scale_all(0, fmod)

    @pl.loop(0, 8)
    def _(i):
        cols = pl.ds(pl.multiple_of(i * 256, 256), 256)
        for k in range(0, FB, 64):
            rows = slice(k, k + 64)
            base = jnp.concatenate([bw[rows], bw[rows]], axis=1)
            target = nT[rows, cols].astype(F32) - sT[rows, cols].astype(F32)
            bt[rows, cols] = (base - target) * (1.0 / math.sqrt(CLIPS * TOK))

    got("s_o")
    stats(o, 0, CB)
    got("s_y")
    stats(y_me, 0, CB)
    forward([(0, 3 * CB)], fresh=True)
    got("xr_vt")
    send_w("xr_vot", v_l, 1, right)
    got("dn_a", "dn_c")
    send("s_u", u, d, "all", sib)
    got("up_b")
    send("s_d", d, u, "all", sib)
    got("s_d")
    stats(u, 0, CB)
    got("s_u")
    stats(d, 0, CB)
    forward([(3 * CB, 2 * CB)])
    got("y_oa", "y_ob")
    send("s_yo", y_o, y_o, "ab", sib)
    got("xr_t", "xl_ot", "xl_vt", "xr_vot")
    sent("xr_t", "xl_t", "pair_t", "xl_ot", "xr_vt", "xl_vt", "xr_vot")
    scale_all(1, tmod)
    got("dn_yab")
    send("s_yu", y_u, y_d, "ab", sib)
    got("up_yab")
    send("s_yd", y_d, y_u, "ab", sib)
    got("s_yo", "s_yd", "s_yu")
    spans = [(b * CB + k, 256) for b in (y_o, y_u, y_d) for k in (0, 384)]
    for first, n in spans:
        stats(0, first, n)
    forward(spans)
    got("dn_yc")
    send("s_yuc", y_u, y_d, "c", sib)
    got("up_yc")
    send("s_ydc", y_d, y_u, "c", sib)
    got("y_oc")
    send("s_yoc", y_o, y_o, "c", sib)
    got("s_yuc", "s_ydc", "s_yoc")

    last = [(b * CB + 256, 128) for b in (y_o, y_u, y_d)]

    @pl.loop(0, 8)
    def _(i):
        cols = pl.ds(pl.multiple_of(i * 256, 256), 256)
        acc[0:FB, cols] += product(0, last, cols)
        for first, n in last:
            add_stats(first, n, cols)
        shift = jnp.sum(st1[:, cols], axis=0, keepdims=True) * (1.0 / (CLIPS * CB))
        power = jnp.sum(st2[:, cols], axis=0, keepdims=True) * (1.0 / (CLIPS * CB))
        mr[0:1, cols] = piv[:, cols] + shift
        mr[1:2, cols] = lax.rsqrt(jnp.maximum(power - shift * shift, 0.0) + EPS)
        m, r = mr[0:1, cols], mr[1:2, cols]
        small = r * (1.0 / math.sqrt(CLIPS * TOK))
        for k in range(0, FB, 64):
            rows = slice(k, k + 64)
            sums = jnp.concatenate([cs[rows], cs[rows]], axis=1)
            err = small * (acc[rows, cols] - sums * m) + bt[rows, cols]
            v = (r * err).astype(BF16)
            vv[rows, cols] = v
            mv = m * v.astype(F32)
            sv[rows, :] += mv[:, :128] + mv[:, 128:]
            sb[rows, :] += err[:, :128] + err[:, 128:]

    sv[...] = jnp.broadcast_to(jnp.sum(sv[...], axis=1, keepdims=True), sv.shape)
    sb[...] = jnp.broadcast_to(jnp.sum(sb[...], axis=1, keepdims=True), sb.shape)

    def grad(block, dst):
        held = slot(block) * CB
        for first, n in ((0, 256), (256, 256), (512, 128)):
            lanes = pl.ds(pl.multiple_of(block * CB + first, 128), n)
            rows = pl.ds(pl.multiple_of(held + first, 128), n)
            part_sum = lax.dot_general(vv[...], at[rows, :], NT, preferred_element_type=F32)
            g = (part_sum - sv[:, 0:1]) * (1.0 + fmod[1:2, lanes]) + sb[:, 0:1] * fmod[0:1, lanes]
            dst[:, first : first + n] = g.astype(dst.dtype)

    HALF = FB // 2
    lo, hi = slice(0, HALF), slice(HALF, FB)
    ls = (1 - l, l)
    for j in (0, 1):
        grad(xo * 2 + ls[j], gopp.at[j])
        copy(f"or{j}", gopp.at[j, lo], ropp.at[0, j], right)
        copy(f"ol{j}", gopp.at[j, hi], ropp.at[1, j], left)
    for j in (0, 1):
        grad(xr * 2 + ls[j], gnb.at[0, j])
        copy(f"rr{j}", gnb.at[0, j, hi], rnb.at[0, j, hi], right)
        grad(xl * 2 + ls[j], gnb.at[1, j])
        copy(f"rl{j}", gnb.at[1, j, lo], rnb.at[1, j, lo], left)
        got(f"or{j}")
        gnb[0, j, lo] = (gnb[0, j, lo].astype(F32) + ropp[0, j].astype(F32)).astype(BF16)
        copy(f"sr{j}", gnb.at[0, j, lo], rnb.at[0, j, lo], right)
        got(f"ol{j}")
        gnb[1, j, hi] = (gnb[1, j, hi].astype(F32) + ropp[1, j].astype(F32)).astype(BF16)
        copy(f"sl{j}", gnb.at[1, j, hi], rnb.at[1, j, hi], left)
    for j in (0, 1):
        grad(x * 2 + ls[j], gown.at[j])

    loads["gen"].wait()

    @pl.loop(0, 8)
    def _(i):
        cols = pl.ds(pl.multiple_of(i * 256, 256), 256)
        acc[FB:CB, cols] = product(FB, [(0, CLIPS * CB)], cols)
        m, r = mr[0:1, cols], mr[1:2, cols]
        for k in range(0, FB, 64):
            rows, more = slice(k, k + 64), slice(FB + k, FB + k + 64)
            own = pl.ds(pl.multiple_of(p * FB + k, 64), 64)

            def twice(ref, where):
                return jnp.concatenate([ref[where], ref[where]], axis=1)

            fv = r * (acc[rows, cols] - twice(cs, rows) * m) + twice(bw, rows)
            tv = r * (acc[more, cols] - twice(cs, more) * m) + twice(bw, more)
            diff = sigma * (tv - fv)
            acc[more, cols] = diff
            away = jnp.abs(
                sT[rows, cols].astype(F32) - (at[own, cols].astype(F32) - sigma * tv)
            )
            pushed = diff * gT[rows, cols].astype(F32)
            col[0, rows, :] += away[:, :128] + away[:, 128:]
            col[1, rows, :] += pushed[:, :128] + pushed[:, 128:]

    total = jnp.sum(jnp.sum(col[0], axis=0, keepdims=True), axis=1, keepdims=True)
    total = jnp.broadcast_to(total, (8, 128))
    for k, to in enumerate(
        (sib, on_f(yh, z + 1 - 2 * (z % 2), p), on_f(yh, 3 - z, p), across)
    ):
        gap_s[k] = total
        copy(f"gap{k}", gap_s.at[k], gap_r.at[k], to)
        got(f"gap{k}")
        total = total + gap_r[k]
    weight = 1.0 / (total[0:1, 0:1] * (1.0 / (TOK * CLIPS * CB)) + EPS)

    same = eye(FB)
    gate_col = jnp.sum(same * gate[...], axis=1, keepdims=True) * weight
    col[0] = jnp.broadcast_to(gate_col, (FB, 128))
    gg_col = jnp.sum(col[1], axis=1, keepdims=True) * weight * (1.0 / math.sqrt(TOK))
    gg_out[...] = jnp.sum(same * gg_col, axis=0, keepdims=True)

    @pl.loop(0, 8)
    def _(i):
        rows = pl.ds(pl.multiple_of(i * 256, 256), 256)
        vv[:, rows] = (col[0, :, 0:1] * acc[FB:CB, rows]).astype(BF16)

    out_bc = pltpu.make_async_copy(vv, bc_out, loc_sems.at[10])
    out_bc.start()

    got("rr0", "sr0", "rl0", "sl0")
    for k, rows in enumerate((lo, hi)):
        gy[rows] = (
            gown[0, rows] + rnb[0, 0, rows].astype(F32) + rnb[1, 0, rows].astype(F32)
        ).astype(BF16)
        copy(f"y{k}", gy.at[rows], ry.at[rows], pair)
    got("rr1", "sr1", "rl1", "sl1")
    gown[1] = gown[1] + rnb[0, 1].astype(F32) + rnb[1, 1].astype(F32)
    got("y0", "y1")
    gown[1] += ry[...].astype(F32)
    out_fg = pltpu.make_async_copy(gown.at[1], fg_out, loc_sems.at[11])
    out_fg.start()
    sent(*table)
    out_bc.wait()
    out_fg.wait()


def per_device(
    sample, noise, gen_branch, step, teacher_mod, fake_mod, teacher_weight, fake_weight, gen_gate
):
    hbm = pl.BlockSpec(memory_space=pl.ANY)
    vmem = pl.BlockSpec(memory_space=pltpu.VMEM)
    cot, gate_grad, grad = pl.pallas_call(
        kernel,
        out_shape=(
            jax.ShapeDtypeStruct((FB, TOK), BF16),
            jax.ShapeDtypeStruct((1, FB), F32),
            jax.ShapeDtypeStruct((FB, CB), F32),
        ),
        in_specs=[
            hbm, hbm, hbm, pl.BlockSpec(memory_space=pltpu.SMEM), vmem, vmem, hbm, hbm, vmem,
        ],
        out_specs=(hbm, vmem, hbm),
        scratch_shapes=[
            pltpu.VMEM((CLIPS * CB, TOK), BF16),
            pltpu.VMEM((CB, CLIPS * CB), BF16),
            pltpu.VMEM((CB, TOK), F32),
            pltpu.VMEM((FB, TOK), BF16),
            pltpu.VMEM((FB, TOK), BF16),
            pltpu.VMEM((FB, TOK), BF16),
            pltpu.VMEM((FB, TOK), BF16),
            pltpu.VMEM((FB, TOK), F32),
            pltpu.VMEM((8, TOK), F32),
            pltpu.VMEM((8, TOK), F32),
            pltpu.VMEM((1, TOK), F32),
            pltpu.VMEM((2, TOK), F32),
            pltpu.VMEM((CB, 128), F32),
            pltpu.VMEM((CB, 128), F32),
            pltpu.VMEM((FB, 128), F32),
            pltpu.VMEM((FB, 128), F32),
            pltpu.VMEM((2, FB, 128), F32),
            pltpu.VMEM((2, FB, CB), BF16),
            pltpu.VMEM((2, 2, FB, CB), BF16),
            pltpu.VMEM((FB, CB), BF16),
            pltpu.VMEM((2, FB, CB), F32),
            pltpu.VMEM((2, 2, FB // 2, CB), BF16),
            pltpu.VMEM((2, 2, FB, CB), BF16),
            pltpu.VMEM((FB, CB), BF16),
            pltpu.VMEM((4, 8, 128), F32),
            pltpu.VMEM((4, 8, 128), F32),
            pltpu.SemaphoreType.DMA((COPIES,)),
            pltpu.SemaphoreType.DMA((COPIES,)),
            pltpu.SemaphoreType.DMA((12,)),
        ],
        compiler_params=pltpu.CompilerParams(
            collective_id=0, has_side_effects=True, vmem_limit_bytes=62 << 20
        ),
        name="step",
    )(
        sample.T, noise.T, gen_branch.T, step,
        teacher_mod.reshape(2, CLIPS * CB), fake_mod.reshape(2, CLIPS * CB),
        teacher_weight.T, fake_weight.T, gen_gate,
    )
    return cot.T, gate_grad, grad.T


def solution(mesh):
    placed = (
        P("clip", "fsdp"),
        P("clip", "fsdp"),
        P("clip", "fsdp"),
        P("clip"),
        P("clip", None, None),
        P("clip", None, None),
        P("clip", "fsdp"),
        P("clip", "fsdp"),
        P("clip", "fsdp"),
    )
    return jax.shard_map(
        per_device,
        mesh=mesh,
        in_specs=placed,
        out_specs=(P("clip", "fsdp"), P("clip", "fsdp"), P("clip", "fsdp")),
        check_vma=False,
    )
```

time: 184 us -> 149 us (0.81)
  Pallas kernels: 168 us -> 143 us
  local copies, waits for them, and re-layouts: 13 us -> 4.06 us
    pallas_call x1, Pallas kernels: 168 us -> 143 us  [per_device(): pl.pallas_call(kernel, out_shape=(jax.ShapeDtypeStruct((FB, TOK), BF16),...]
    unnamed x16 -> x7, local copies, waits for them, and re-layouts: 9.22 us -> 4.06 us
    pallas_call x2 -> x0, local copies, waits for them, and re-layouts: 3.79 us -> none  [per_device(): pl.pallas_call(kernel, out_shape=(jax.ShapeDtypeStruct((TOK, FB), BF16),...]
where the time goes in v2:
time: 149 us; the launch traced here: 148 us
  Pallas kernels  143 us (96%)
  local copies, waits for them, and re-layouts  4.06 us (3%)
    pallas_call x1, Pallas kernels, per_device(): pl.pallas_call(kernel, out_shape=(jax.ShapeDtypeStruct((FB, TOK), BF16),...  143 us
    unnamed x7, local copies, waits for them, and re-layouts  4.06 us

profile of v2, /device:TPU:1, one launch (start us, length us, event | category | flops | bytes accessed | tf_op | source)
XLA Modules:
  0.0 148.1 jit_solution(8203590848841163411)
XLA Ops:
  1.3 142.7 %step.2 = (bf16[320,2048]{1,0:T(8,128)(2,1)}, f32[1,320]{1,0:T(1,128)}, f32[320,640]{1,0:T(8,128)}) custom-call(bf16[320,2048]{1,0:T(8,128)(2,1)} %bitcast.10, bf16[320,2048]{1,0:T(8,128)(2,1)} %bitcast.11, bf16[320,2048]{1,0:T(8,128)(2,1)} %bitcast.12, s32[1]{0:T(128)S(6)} %copy.15.step, f32[2,5120]{1,0:T(2,128)} %bitcast.16, f32[2,5120]{1,0:T(2,128)} %bitcast.17, ...), custom_call_target="tpu_custom_call" | custom-call | tf_op jit(solution)/shard_map/step/pallas_call | solution.py:445
  144.0 0.0 copy-start.1
  144.0 0.0 copy-start
  144.0 2.6 %copy.16 = bf16[2048,320]{0,1:T(8,128)(2,1)} copy(bf16[2048,320]{0,1:T(8,128)(2,1)} %bitcast.9) | data formatting | bytes 2621440
  146.6 0.0 copy-done.1
  146.6 0.6 copy.17
  147.2 0.0 copy-done
  147.2 0.9 copy.18
Async XLA Ops:
  144.0 2.6 %copy-start.1 = (f32[1,320]{1,0:T(1,128)S(1)}, f32[1,320]{1,0:T(1,128)}, u32[]{:S(2)}) copy-start(f32[1,320]{1,0:T(1,128)} %get-tuple-element.13) | copy-start | bytes 3844
  144.0 3.2 %copy-start = (f32[320,640]{1,0:T(8,128)S(1)}, f32[320,640]{1,0:T(8,128)}, u32[]{:S(2)}) copy-start(f32[320,640]{1,0:T(8,128)} %get-tuple-element.8) | copy-start | bytes 2457604

commit v3 on v2

--- a/solution.py
+++ b/solution.py
@@ -17,7 +17,7 @@
 FB = 320
 CB = 640
 CLIPS = 8
-COPIES = 64
+COPIES = 80
 
 
 def eye(n):
@@ -26,10 +26,10 @@
 
 
 def kernel(
-    sample, noise, gen, step, tmod, fmod, tw, fw, gate,
+    sample, noise, gen, step, tmod_in, fmod_in, tw, fw, gate_in,
     bc_out, gg_out, fg_out,
     at, wt, acc, sT, nT, gT, vv, bt, st1, st2, piv, mr, cs, bw, sv, sb, col,
-    gopp, gnb, gy, gown, ropp, rnb, ry, gap_s, gap_r,
+    tmod, fmod, gate, g, gown, rpo, rpn, ryq, rqo, rqn, rpy, gap_s, gap_r,
     send_sems, recv_sems, loc_sems,
 ):
     clip = lax.axis_index("clip")
@@ -116,7 +116,10 @@
         load("n" + which, noise.at[local(which), :], nT.at[local(which), :])
     load("fw", fw, w_ref(clip, 0))
     load("tw", tw, w_ref(clip, 1))
+    load("fmod", fmod_in, fmod)
+    load("tmod", tmod_in, tmod)
     load("gen", gen, gT)
+    load("gate", gate_in, gate)
     barrier = pltpu.get_barrier_semaphore()
     for to in (up, dn, across, sib, right, left, pair):
         pl.semaphore_signal(barrier, inc=1, device_id=to, device_id_type=pl.DeviceIdType.MESH)
@@ -217,14 +220,14 @@
             preferred_element_type=F32,
         )
 
-    def forward(spans, fresh=False):
+    def forward(spans, fresh=False, top=0):
         @pl.loop(0, 8)
         def _(i):
             cols = pl.ds(pl.multiple_of(i * 256, 256), 256)
             if fresh:
-                acc[0:FB, cols] = product(0, spans, cols)
+                acc[top : top + FB, cols] = product(top, spans, cols)
             else:
-                acc[0:FB, cols] += product(0, spans, cols)
+                acc[top : top + FB, cols] += product(top, spans, cols)
 
     got("xr_f")
     send_w("xr_of", w_l, 0, right)
@@ -264,6 +267,7 @@
     send_w("xl_vt", v_me, 1, left)
     got("xl_f", "xr_of", "xr_vf", "xl_vof")
     sent("xr_f", "xl_f", "pair_f", "xr_of", "xr_vf", "xl_vf", "xl_vof")
+    loads["fmod"].wait()
     scale_all(0, fmod)
 
     @pl.loop(0, 8)
@@ -295,7 +299,9 @@
     send("s_yo", y_o, y_o, "ab", sib)
     got("xr_t", "xl_ot", "xl_vt", "xr_vot")
     sent("xr_t", "xl_t", "pair_t", "xl_ot", "xr_vt", "xl_vt", "xr_vot")
+    loads["tmod"].wait()
     scale_all(1, tmod)
+    forward([(0, 5 * CB)], True, FB)
     got("dn_yab")
     send("s_yu", y_u, y_d, "ab", sib)
     got("up_yab")
@@ -349,61 +355,104 @@
             g = (part_sum - sv[:, 0:1]) * (1.0 + fmod[1:2, lanes]) + sb[:, 0:1] * fmod[0:1, lanes]
             dst[:, first : first + n] = g.astype(dst.dtype)
 
-    HALF = FB // 2
-    lo, hi = slice(0, HALF), slice(HALF, FB)
+    P_ROWS, P_A, P_B = slice(0, 192), slice(0, 96), slice(96, 192)
+    Q_ROWS, Q_A, Q_B = slice(192, 320), slice(192, 256), slice(256, 320)
     ls = (1 - l, l)
-    for j in (0, 1):
-        grad(xo * 2 + ls[j], gopp.at[j])
-        copy(f"or{j}", gopp.at[j, lo], ropp.at[0, j], right)
-        copy(f"ol{j}", gopp.at[j, hi], ropp.at[1, j], left)
-    for j in (0, 1):
-        grad(xr * 2 + ls[j], gnb.at[0, j])
-        copy(f"rr{j}", gnb.at[0, j, hi], rnb.at[0, j, hi], right)
-        grad(xl * 2 + ls[j], gnb.at[1, j])
-        copy(f"rl{j}", gnb.at[1, j, lo], rnb.at[1, j, lo], left)
+
+    def add(dst, rows, *terms):
+        dst[rows] = sum([t.astype(F32) for t in terms], dst[rows].astype(F32)).astype(dst.dtype)
+
+    def opposite(j):
+        grad(xo * 2 + ls[j], g.at[0, j])
+        copy(f"or{j}", g.at[0, j, P_A], rpo.at[0, j], right)
+        copy(f"ol{j}", g.at[0, j, P_B], rpo.at[1, j], left)
+
+    def next_one(j):
+        grad(xr * 2 + ls[j], g.at[1, j])
+        copy(f"rr{j}", g.at[1, j, P_B], rpn.at[0, j, P_B], right)
+        if j == 0:
+            copy("q1", g.at[1, 0, Q_ROWS], ryq.at[1], pair)
+        grad(xl * 2 + ls[j], g.at[2, j])
+        copy(f"rl{j}", g.at[2, j, P_A], rpn.at[1, j, P_A], left)
+        if j == 0:
+            copy("q2", g.at[2, 0, Q_ROWS], ryq.at[2], pair)
+
+    def pass_on(j):
         got(f"or{j}")
-        gnb[0, j, lo] = (gnb[0, j, lo].astype(F32) + ropp[0, j].astype(F32)).astype(BF16)
-        copy(f"sr{j}", gnb.at[0, j, lo], rnb.at[0, j, lo], right)
+        add(g.at[1, j], P_A, rpo[0, j])
+        copy(f"sr{j}", g.at[1, j, P_A], rpn.at[0, j, P_A], right)
         got(f"ol{j}")
-        gnb[1, j, hi] = (gnb[1, j, hi].astype(F32) + ropp[1, j].astype(F32)).astype(BF16)
-        copy(f"sl{j}", gnb.at[1, j, hi], rnb.at[1, j, hi], left)
-    for j in (0, 1):
-        grad(x * 2 + ls[j], gown.at[j])
+        add(g.at[2, j], P_B, rpo[1, j])
+        copy(f"sl{j}", g.at[2, j, P_B], rpn.at[1, j, P_B], left)
+
+    opposite(0)
+    copy("q0", g.at[0, 0, Q_ROWS], ryq.at[0], pair)
+    opposite(1)
+    next_one(0)
+    pass_on(0)
+    next_one(1)
+    got("q0")
+    add(g.at[0, 1], Q_ROWS, ryq[0])
+    copy("hor", g.at[0, 1, Q_A], rqo.at[0], right)
+    copy("hol", g.at[0, 1, Q_B], rqo.at[1], left)
+    pass_on(1)
+    grad(x * 2 + ls[0], gown.at[0])
+    g[3, 0, Q_ROWS] = gown[0, Q_ROWS].astype(BF16)
+    copy("q3", g.at[3, 0, Q_ROWS], ryq.at[3], pair)
+    grad(x * 2 + ls[1], gown.at[1])
 
     loads["gen"].wait()
-
-    @pl.loop(0, 8)
-    def _(i):
-        cols = pl.ds(pl.multiple_of(i * 256, 256), 256)
-        acc[FB:CB, cols] = product(FB, [(0, CLIPS * CB)], cols)
-        m, r = mr[0:1, cols], mr[1:2, cols]
-        for k in range(0, FB, 64):
-            rows, more = slice(k, k + 64), slice(FB + k, FB + k + 64)
-            own = pl.ds(pl.multiple_of(p * FB + k, 64), 64)
-
-            def twice(ref, where):
-                return jnp.concatenate([ref[where], ref[where]], axis=1)
-
-            fv = r * (acc[rows, cols] - twice(cs, rows) * m) + twice(bw, rows)
-            tv = r * (acc[more, cols] - twice(cs, more) * m) + twice(bw, more)
-            diff = sigma * (tv - fv)
-            acc[more, cols] = diff
-            away = jnp.abs(
-                sT[rows, cols].astype(F32) - (at[own, cols].astype(F32) - sigma * tv)
-            )
-            pushed = diff * gT[rows, cols].astype(F32)
-            col[0, rows, :] += away[:, :128] + away[:, 128:]
-            col[1, rows, :] += pushed[:, :128] + pushed[:, 128:]
+    loads["gate"].wait()
+
+    def teacher(first, last):
+        @pl.loop(first, last)
+        def _(i):
+            cols = pl.ds(pl.multiple_of(i * 256, 256), 256)
+            acc[FB:CB, cols] += product(FB, [(5 * CB, 3 * CB)], cols)
+            m, r = mr[0:1, cols], mr[1:2, cols]
+            for k in range(0, FB, 64):
+                rows, more = slice(k, k + 64), slice(FB + k, FB + k + 64)
+                own = pl.ds(pl.multiple_of(p * FB + k, 64), 64)
+
+                def twice(ref, where):
+                    return jnp.concatenate([ref[where], ref[where]], axis=1)
+
+                fv = r * (acc[rows, cols] - twice(cs, rows) * m) + twice(bw, rows)
+                tv = r * (acc[more, cols] - twice(cs, more) * m) + twice(bw, more)
+                diff = sigma * (tv - fv)
+                acc[more, cols] = diff
+                away = jnp.abs(
+                    sT[rows, cols].astype(F32) - (at[own, cols].astype(F32) - sigma * tv)
+                )
+                pushed = diff * gT[rows, cols].astype(F32)
+                col[0, rows, :] += away[:, :128] + away[:, 128:]
+                col[1, rows, :] += pushed[:, :128] + pushed[:, 128:]
+
+    teacher(0, 4)
+    got("q1", "hor")
+    add(g.at[1, 1], Q_ROWS, ryq[1])
+    add(g.at[1, 1], Q_A, rqo[0])
+    copy("hr", g.at[1, 1, Q_ROWS], rqn.at[0], right)
+    got("q2", "hol")
+    add(g.at[2, 1], Q_ROWS, ryq[2])
+    add(g.at[2, 1], Q_B, rqo[1])
+    copy("hl", g.at[2, 1, Q_ROWS], rqn.at[1], left)
+    teacher(4, 8)
 
     total = jnp.sum(jnp.sum(col[0], axis=0, keepdims=True), axis=1, keepdims=True)
-    total = jnp.broadcast_to(total, (8, 128))
-    for k, to in enumerate(
-        (sib, on_f(yh, z + 1 - 2 * (z % 2), p), on_f(yh, 3 - z, p), across)
-    ):
-        gap_s[k] = total
-        copy(f"gap{k}", gap_s.at[k], gap_r.at[k], to)
+    gap_s[0] = jnp.broadcast_to(total, (8, 128))
+    copy("gap0", gap_s.at[0], gap_r.at[0], sib)
+    got("rr0", "sr0", "rl0", "sl0")
+    g[3, 0, P_ROWS] = (
+        gown[0, P_ROWS] + rpn[0, 0].astype(F32) + rpn[1, 0].astype(F32)
+    ).astype(BF16)
+    copy("py", g.at[3, 0, P_ROWS], rpy, pair)
+    for k, to in enumerate((on_f(yh, z + 1 - 2 * (z % 2), p), on_f(yh, 3 - z, p), across)):
         got(f"gap{k}")
-        total = total + gap_r[k]
+        gap_s[k + 1] = gap_s[k] + gap_r[k]
+        copy(f"gap{k + 1}", gap_s.at[k + 1], gap_r.at[k + 1], to)
+    got("gap3")
+    total = gap_s[3] + gap_r[3]
     weight = 1.0 / (total[0:1, 0:1] * (1.0 / (TOK * CLIPS * CB)) + EPS)
 
     same = eye(FB)
@@ -417,20 +466,16 @@
         rows = pl.ds(pl.multiple_of(i * 256, 256), 256)
         vv[:, rows] = (col[0, :, 0:1] * acc[FB:CB, rows]).astype(BF16)
 
-    out_bc = pltpu.make_async_copy(vv, bc_out, loc_sems.at[10])
+    out_bc = pltpu.make_async_copy(vv, bc_out, loc_sems.at[13])
     out_bc.start()
 
-    got("rr0", "sr0", "rl0", "sl0")
-    for k, rows in enumerate((lo, hi)):
-        gy[rows] = (
-            gown[0, rows] + rnb[0, 0, rows].astype(F32) + rnb[1, 0, rows].astype(F32)
-        ).astype(BF16)
-        copy(f"y{k}", gy.at[rows], ry.at[rows], pair)
     got("rr1", "sr1", "rl1", "sl1")
-    gown[1] = gown[1] + rnb[0, 1].astype(F32) + rnb[1, 1].astype(F32)
-    got("y0", "y1")
-    gown[1] += ry[...].astype(F32)
-    out_fg = pltpu.make_async_copy(gown.at[1], fg_out, loc_sems.at[11])
+    add(gown.at[1], P_ROWS, rpn[0, 1], rpn[1, 1])
+    got("q3", "hr", "hl")
+    add(gown.at[1], Q_ROWS, ryq[3], rqn[0], rqn[1])
+    got("py")
+    add(gown.at[1], P_ROWS, rpy[...])
+    out_fg = pltpu.make_async_copy(gown.at[1], fg_out, loc_sems.at[14])
     out_fg.start()
     sent(*table)
     out_bc.wait()
@@ -450,7 +495,7 @@
             jax.ShapeDtypeStruct((FB, CB), F32),
         ),
         in_specs=[
-            hbm, hbm, hbm, pl.BlockSpec(memory_space=pltpu.SMEM), vmem, vmem, hbm, hbm, vmem,
+            hbm, hbm, hbm, pl.BlockSpec(memory_space=pltpu.SMEM), hbm, hbm, hbm, hbm, hbm,
         ],
         out_specs=(hbm, vmem, hbm),
         scratch_shapes=[
@@ -471,18 +516,22 @@
             pltpu.VMEM((FB, 128), F32),
             pltpu.VMEM((FB, 128), F32),
             pltpu.VMEM((2, FB, 128), F32),
-            pltpu.VMEM((2, FB, CB), BF16),
-            pltpu.VMEM((2, 2, FB, CB), BF16),
-            pltpu.VMEM((FB, CB), BF16),
+            pltpu.VMEM((2, CLIPS * CB), F32),
+            pltpu.VMEM((2, CLIPS * CB), F32),
+            pltpu.VMEM((1, FB), F32),
+            pltpu.VMEM((4, 2, FB, CB), BF16),
             pltpu.VMEM((2, FB, CB), F32),
-            pltpu.VMEM((2, 2, FB // 2, CB), BF16),
-            pltpu.VMEM((2, 2, FB, CB), BF16),
-            pltpu.VMEM((FB, CB), BF16),
+            pltpu.VMEM((2, 2, 96, CB), BF16),
+            pltpu.VMEM((2, 2, 192, CB), BF16),
+            pltpu.VMEM((4, 128, CB), BF16),
+            pltpu.VMEM((2, 64, CB), BF16),
+            pltpu.VMEM((2, 128, CB), BF16),
+            pltpu.VMEM((192, CB), BF16),
             pltpu.VMEM((4, 8, 128), F32),
             pltpu.VMEM((4, 8, 128), F32),
             pltpu.SemaphoreType.DMA((COPIES,)),
             pltpu.SemaphoreType.DMA((COPIES,)),
-            pltpu.SemaphoreType.DMA((12,)),
+            pltpu.SemaphoreType.DMA((15,)),
         ],
         compiler_params=pltpu.CompilerParams(
             collective_id=0, has_side_effects=True, vmem_limit_bytes=62 << 20

time: 149 us -> 143 us (0.960)
  Pallas kernels: 143 us -> 137 us
    pallas_call x1, Pallas kernels: 143 us -> 137 us  [per_device(): pl.pallas_call(kernel, out_shape=(jax.ShapeDtypeStruct((FB, TOK), BF16),...]
where the time goes in v3:
time: 143 us; the launch traced here: 142 us
  Pallas kernels  137 us (96%)
  local copies, waits for them, and re-layouts  4.06 us (3%)
    pallas_call x1, Pallas kernels, per_device(): pl.pallas_call(kernel, out_shape=(jax.ShapeDtypeStruct((FB, TOK), BF16),...  137 us
    unnamed x7, local copies, waits for them, and re-layouts  4.06 us

profile of v3, /device:TPU:1, one launch (start us, length us, event | category | flops | bytes accessed | tf_op | source)
XLA Modules:
  0.0 142.4 jit_solution(32323707889785986)
XLA Ops:
  1.3 137.0 %step.2 = (bf16[320,2048]{1,0:T(8,128)(2,1)}, f32[1,320]{1,0:T(1,128)}, f32[320,640]{1,0:T(8,128)}) custom-call(bf16[320,2048]{1,0:T(8,128)(2,1)} %bitcast.10, bf16[320,2048]{1,0:T(8,128)(2,1)} %bitcast.11, bf16[320,2048]{1,0:T(8,128)(2,1)} %bitcast.12, s32[1]{0:T(128)S(6)} %copy.15.step, f32[2,5120]{1,0:T(2,128)} %bitcast.16, f32[2,5120]{1,0:T(2,128)} %bitcast.17, ...), custom_call_target="tpu_custom_call" | custom-call | tf_op jit(solution)/shard_map/step/pallas_call | solution.py:490
  138.3 0.0 copy-start.1
  138.3 0.0 copy-start
  138.3 2.6 %copy.16 = bf16[2048,320]{0,1:T(8,128)(2,1)} copy(bf16[2048,320]{0,1:T(8,128)(2,1)} %bitcast.9) | data formatting | bytes 2621440
  140.9 0.0 copy-done.1
  140.9 0.6 copy.17
  141.5 0.0 copy-done
  141.5 0.9 copy.18
Async XLA Ops:
  138.3 2.6 %copy-start.1 = (f32[1,320]{1,0:T(1,128)S(1)}, f32[1,320]{1,0:T(1,128)}, u32[]{:S(2)}) copy-start(f32[1,320]{1,0:T(1,128)} %get-tuple-element.13) | copy-start | bytes 3844
  138.3 3.2 %copy-start = (f32[320,640]{1,0:T(8,128)S(1)}, f32[320,640]{1,0:T(8,128)}, u32[]{:S(2)}) copy-start(f32[320,640]{1,0:T(8,128)} %get-tuple-element.8) | copy-start | bytes 2457604

commit v4 on v3

--- a/solution.py
+++ b/solution.py
@@ -29,7 +29,7 @@
     sample, noise, gen, step, tmod_in, fmod_in, tw, fw, gate_in,
     bc_out, gg_out, fg_out,
     at, wt, acc, sT, nT, gT, vv, bt, st1, st2, piv, mr, cs, bw, sv, sb, col,
-    tmod, fmod, gate, g, gown, rpo, rpn, ryq, rqo, rqn, rpy, gap_s, gap_r,
+    tmod, fmod, gate, g, gown, rpo, rpn, ryq, rqo, rqn, rpy, stat_s, stat_r, gap_s, gap_r,
     send_sems, recv_sems, loc_sems,
 ):
     clip = lax.axis_index("clip")
@@ -146,6 +146,8 @@
     send("dn_b", me, u, "b", dn)
     loads["fw"].wait()
     send_w("pair_f", clip, 0, pair)
+    loads["tw"].wait()
+    send_w("pair_t", clip, 1, pair)
     send("y_ab", me, y_me, "ab", across)
     send_w("xr_f", clip, 0, right)
     send_w("xl_f", clip, 0, left)
@@ -154,10 +156,8 @@
     send("dn_a", me, u, "a", dn)
     send("y_c", me, y_me, "c", across)
     send("s_own", me, me, "all", sib)
-    loads["tw"].wait()
     send_w("xr_t", clip, 1, right)
     send_w("xl_t", clip, 1, left)
-    send_w("pair_t", clip, 1, pair)
 
     w_l, w_r, w_o = xl * 2 + l, xr * 2 + l, xo * 2 + l
     v_me, v_l, v_r, v_o = x * 2 + 1 - l, xl * 2 + 1 - l, xr * 2 + 1 - l, xo * 2 + 1 - l
@@ -178,15 +178,17 @@
     col[...] = jnp.zeros_like(col)
 
     def add_stats(first, n, cols):
-        v = at[first : first + n, cols].astype(F32) - piv[:, cols]
+        v = at[pl.ds(first, n), cols].astype(F32) - piv[:, cols]
         v = v.reshape(n // 8, 8, 256)
         st1[:, cols] += jnp.sum(v, axis=0)
         st2[:, cols] += jnp.sum(v * v, axis=0)
 
-    def stats(block, first, n):
+    def stats(block, which):
+        first, n = part[which]
+
         @pl.loop(0, 8)
         def _(i):
-            add_stats(block * CB + first, n, pl.ds(pl.multiple_of(i * 256, 256), 256))
+            add_stats(pl.multiple_of(block * CB + first, 64), n, pl.ds(pl.multiple_of(i * 256, 256), 256))
 
     def scale(block, h, mod):
         lanes = pl.ds(pl.multiple_of(block * CB, 128), CB)
@@ -242,8 +244,7 @@
     got("up_c")
     send("up_oc", d, o, "c", up)
     send("up_b", me, d, "b", up)
-    got("s_own")
-    stats(me, 0, CB)
+    stats(me, "all")
     got("xl_vf")
     send_w("xl_vof", v_r, 0, left)
     got("xl_t")
@@ -279,10 +280,9 @@
             target = nT[rows, cols].astype(F32) - sT[rows, cols].astype(F32)
             bt[rows, cols] = (base - target) * (1.0 / math.sqrt(CLIPS * TOK))
 
-    got("s_o")
-    stats(o, 0, CB)
-    got("s_y")
-    stats(y_me, 0, CB)
+    stats(o, "all")
+    stats(y_me, "all")
+    got("s_own", "s_o", "s_y")
     forward([(0, 3 * CB)], fresh=True)
     got("xr_vt")
     send_w("xr_vot", v_l, 1, right)
@@ -290,13 +290,10 @@
     send("s_u", u, d, "all", sib)
     got("up_b")
     send("s_d", d, u, "all", sib)
-    got("s_d")
-    stats(u, 0, CB)
-    got("s_u")
-    stats(d, 0, CB)
+    stats(u, "all")
+    stats(d, "all")
+    got("s_d", "s_u")
     forward([(3 * CB, 2 * CB)])
-    got("y_oa", "y_ob")
-    send("s_yo", y_o, y_o, "ab", sib)
     got("xr_t", "xl_ot", "xl_vt", "xr_vot")
     sent("xr_t", "xl_t", "pair_t", "xl_ot", "xr_vt", "xl_vt", "xr_vot")
     loads["tmod"].wait()
@@ -306,11 +303,28 @@
     send("s_yu", y_u, y_d, "ab", sib)
     got("up_yab")
     send("s_yd", y_d, y_u, "ab", sib)
-    got("s_yo", "s_yd", "s_yu")
-    spans = [(b * CB + k, 256) for b in (y_o, y_u, y_d) for k in (0, 384)]
-    for first, n in spans:
-        stats(0, first, n)
-    forward(spans)
+    stats(y_u, "ab")
+    stats(y_d, "ab")
+    got("s_yd", "s_yu")
+    forward([(b * CB + k, 256) for b in (y_u, y_d) for k in (0, 384)])
+    got("y_oa", "y_ob")
+    send("s_yo", y_o, y_o, "ab", sib)
+    stats(y_o, "ab")
+
+    held = 5 * FB + 3 * 256
+    shift = jnp.sum(st1[...], axis=0, keepdims=True)
+    stat_s[0:1, :] = piv[...] + shift * (1.0 / held)
+    stat_s[1:2, :] = jnp.sum(st2[...], axis=0, keepdims=True) - shift * shift * (1.0 / held)
+    copy("stat", stat_s, stat_r, sib)
+    got("s_yo")
+    forward([(y_o * CB + k, 256) for k in (0, 384)])
+    got("stat")
+    apart = stat_s[0:1, :] - stat_r[0:1, :]
+    piv[...] = 0.5 * (stat_s[0:1, :] + stat_r[0:1, :])
+    power_held = stat_s[1:2, :] + stat_r[1:2, :] + apart * apart * (held / 2)
+    st1[...] = jnp.zeros_like(st1)
+    st2[...] = jnp.broadcast_to(power_held * 0.125, st2.shape)
+
     got("dn_yc")
     send("s_yuc", y_u, y_d, "c", sib)
     got("up_yc")
@@ -399,7 +413,6 @@
     grad(x * 2 + ls[0], gown.at[0])
     g[3, 0, Q_ROWS] = gown[0, Q_ROWS].astype(BF16)
     copy("q3", g.at[3, 0, Q_ROWS], ryq.at[3], pair)
-    grad(x * 2 + ls[1], gown.at[1])
 
     loads["gen"].wait()
     loads["gate"].wait()
@@ -428,29 +441,35 @@
                 col[0, rows, :] += away[:, :128] + away[:, 128:]
                 col[1, rows, :] += pushed[:, :128] + pushed[:, 128:]
 
-    teacher(0, 4)
+    teacher(0, 8)
+    total = jnp.sum(jnp.sum(col[0], axis=0, keepdims=True), axis=1, keepdims=True)
+    gap_s[0] = jnp.broadcast_to(total, (8, 128))
+    gap_to = (sib, on_f(yh, z + 1 - 2 * (z % 2), p), on_f(yh, 3 - z, p), across)
+
+    def gap_step(k):
+        if k:
+            got(f"gap{k - 1}")
+            gap_s[k] = gap_s[k - 1] + gap_r[k - 1]
+        copy(f"gap{k}", gap_s.at[k], gap_r.at[k], gap_to[k])
+
+    gap_step(0)
     got("q1", "hor")
     add(g.at[1, 1], Q_ROWS, ryq[1])
     add(g.at[1, 1], Q_A, rqo[0])
     copy("hr", g.at[1, 1, Q_ROWS], rqn.at[0], right)
+    gap_step(1)
     got("q2", "hol")
     add(g.at[2, 1], Q_ROWS, ryq[2])
     add(g.at[2, 1], Q_B, rqo[1])
     copy("hl", g.at[2, 1, Q_ROWS], rqn.at[1], left)
-    teacher(4, 8)
-
-    total = jnp.sum(jnp.sum(col[0], axis=0, keepdims=True), axis=1, keepdims=True)
-    gap_s[0] = jnp.broadcast_to(total, (8, 128))
-    copy("gap0", gap_s.at[0], gap_r.at[0], sib)
+    gap_step(2)
     got("rr0", "sr0", "rl0", "sl0")
     g[3, 0, P_ROWS] = (
         gown[0, P_ROWS] + rpn[0, 0].astype(F32) + rpn[1, 0].astype(F32)
     ).astype(BF16)
     copy("py", g.at[3, 0, P_ROWS], rpy, pair)
-    for k, to in enumerate((on_f(yh, z + 1 - 2 * (z % 2), p), on_f(yh, 3 - z, p), across)):
-        got(f"gap{k}")
-        gap_s[k + 1] = gap_s[k] + gap_r[k]
-        copy(f"gap{k + 1}", gap_s.at[k + 1], gap_r.at[k + 1], to)
+    gap_step(3)
+    grad(x * 2 + ls[1], gown.at[1])
     got("gap3")
     total = gap_s[3] + gap_r[3]
     weight = 1.0 / (total[0:1, 0:1] * (1.0 / (TOK * CLIPS * CB)) + EPS)
@@ -527,6 +546,8 @@
             pltpu.VMEM((2, 64, CB), BF16),
             pltpu.VMEM((2, 128, CB), BF16),
             pltpu.VMEM((192, CB), BF16),
+            pltpu.VMEM((2, TOK), F32),
+            pltpu.VMEM((2, TOK), F32),
             pltpu.VMEM((4, 8, 128), F32),
             pltpu.VMEM((4, 8, 128), F32),
             pltpu.SemaphoreType.DMA((COPIES,)),

time: 143 us -> 136 us (0.951)
  Pallas kernels: 137 us -> 130 us
    pallas_call x1, Pallas kernels: 137 us -> 130 us  [per_device(): pl.pallas_call(kernel, out_shape=(jax.ShapeDtypeStruct((FB, TOK), BF16),...]
where the time goes in v4:
time: 136 us
  Pallas kernels  130 us (96%)
  local copies, waits for them, and re-layouts  4.06 us (3%)
    pallas_call x1, Pallas kernels, per_device(): pl.pallas_call(kernel, out_shape=(jax.ShapeDtypeStruct((FB, TOK), BF16),...  130 us
    unnamed x7, local copies, waits for them, and re-layouts  4.06 us

profile of v4, /device:TPU:1, one launch (start us, length us, event | category | flops | bytes accessed | tf_op | source)
XLA Modules:
  0.0 135.8 jit_solution(3638774420263169323)
XLA Ops:
  1.3 130.5 %step.2 = (bf16[320,2048]{1,0:T(8,128)(2,1)}, f32[1,320]{1,0:T(1,128)}, f32[320,640]{1,0:T(8,128)}) custom-call(bf16[320,2048]{1,0:T(8,128)(2,1)} %bitcast.10, bf16[320,2048]{1,0:T(8,128)(2,1)} %bitcast.11, bf16[320,2048]{1,0:T(8,128)(2,1)} %bitcast.12, s32[1]{0:T(128)S(6)} %copy.15.step, f32[2,5120]{1,0:T(2,128)} %bitcast.16, f32[2,5120]{1,0:T(2,128)} %bitcast.17, ...), custom_call_target="tpu_custom_call" | custom-call | tf_op jit(solution)/shard_map/step/pallas_call | solution.py:509
  131.8 0.0 copy-start.1
  131.8 0.0 copy-start
  131.8 2.6 %copy.16 = bf16[2048,320]{0,1:T(8,128)(2,1)} copy(bf16[2048,320]{0,1:T(8,128)(2,1)} %bitcast.9) | data formatting | bytes 2621440
  134.4 0.0 copy-done.1
  134.4 0.6 copy.17
  134.9 0.0 copy-done
  134.9 0.9 copy.18
Async XLA Ops:
  131.8 2.6 %copy-start.1 = (f32[1,320]{1,0:T(1,128)S(1)}, f32[1,320]{1,0:T(1,128)}, u32[]{:S(2)}) copy-start(f32[1,320]{1,0:T(1,128)} %get-tuple-element.13) | copy-start | bytes 3844
  131.8 3.2 %copy-start = (f32[320,640]{1,0:T(8,128)S(1)}, f32[320,640]{1,0:T(8,128)}, u32[]{:S(2)}) copy-start(f32[320,640]{1,0:T(8,128)} %get-tuple-element.8) | copy-start | bytes 2457604

commit v5 on v4

--- a/solution.py
+++ b/solution.py
@@ -49,13 +49,12 @@
 
     up, dn, across, sib = on_f(yh, zu, p), on_f(yh, zd, p), on_f(yo, z, p), on_f(yh, z, 1 - p)
     right, left, pair = on_c(xr, l), on_c(xl, l), on_c(x, 1 - l)
-    me, y_me, o, u, d, y_o, y_u, y_d = range(8)
+    me, o, u, d, y_me, y_o, y_u, y_d = range(8)
 
     def slot(block):
         rel = ((block % 4 - z) * s + 8) % 4
-        r1, r2 = rel % 2, rel // 2
         yd = (block // 4 + yh) % 2
-        return (1 - r1) * (yd + (2 + 2 * yd) * r2) + r1 * (3 + 3 * yd + r2)
+        return yd * 4 + (rel % 2) * 2 + rel // 2
 
     table = {}
 
@@ -233,25 +232,25 @@
 
     got("xr_f")
     send_w("xr_of", w_l, 0, right)
-    got("pair_f")
-    send_w("xr_vf", v_me, 0, right)
-    send_w("xl_vf", v_me, 0, left)
     got("up_a")
     send("up_oa", d, o, "a", up)
     got("dn_b")
     send("dn_ob", u, o, "b", dn)
     send("dn_c", me, u, "c", dn)
+    got("pair_f")
+    send_w("xr_vf", v_me, 0, right)
+    send_w("xl_vf", v_me, 0, left)
     got("up_c")
     send("up_oc", d, o, "c", up)
     send("up_b", me, d, "b", up)
+    got("pair_t")
+    send_w("xr_vt", v_me, 1, right)
     stats(me, "all")
     got("xl_vf")
     send_w("xl_vof", v_r, 0, left)
+    send_w("xl_vt", v_me, 1, left)
     got("xl_t")
     send_w("xl_ot", w_r, 1, left)
-    got("y_ab")
-    send("up_yab", y_me, y_d, "ab", up)
-    send("dn_yab", y_me, y_u, "ab", dn)
     got("up_oa")
     send("y_oa", o, y_o, "a", across)
     got("dn_ob")
@@ -259,17 +258,13 @@
     got("up_oc")
     send("y_oc", o, y_o, "c", across)
     send("s_o", o, o, "all", sib)
-    got("y_c")
-    send("up_yc", y_me, y_d, "c", up)
-    send("dn_yc", y_me, y_u, "c", dn)
-    send("s_y", y_me, y_me, "all", sib)
-    got("pair_t")
-    send_w("xr_vt", v_me, 1, right)
-    send_w("xl_vt", v_me, 1, left)
     got("xl_f", "xr_of", "xr_vf", "xl_vof")
     sent("xr_f", "xl_f", "pair_f", "xr_of", "xr_vf", "xl_vf", "xl_vof")
     loads["fmod"].wait()
     scale_all(0, fmod)
+    got("y_ab")
+    send("up_yab", y_me, y_d, "ab", up)
+    send("dn_yab", y_me, y_u, "ab", dn)
 
     @pl.loop(0, 8)
     def _(i):
@@ -280,20 +275,24 @@
             target = nT[rows, cols].astype(F32) - sT[rows, cols].astype(F32)
             bt[rows, cols] = (base - target) * (1.0 / math.sqrt(CLIPS * TOK))
 
-    stats(o, "all")
-    stats(y_me, "all")
-    got("s_own", "s_o", "s_y")
-    forward([(0, 3 * CB)], fresh=True)
+    got("s_own", "s_o")
+    forward([(0, 2 * CB)], fresh=True)
     got("xr_vt")
     send_w("xr_vot", v_l, 1, right)
     got("dn_a", "dn_c")
     send("s_u", u, d, "all", sib)
+    stats(o, "all")
     got("up_b")
     send("s_d", d, u, "all", sib)
+    got("y_c")
+    send("up_yc", y_me, y_d, "c", up)
+    send("dn_yc", y_me, y_u, "c", dn)
+    send("s_y", y_me, y_me, "all", sib)
     stats(u, "all")
     stats(d, "all")
-    got("s_d", "s_u")
-    forward([(3 * CB, 2 * CB)])
+    got("s_d", "s_u", "s_y")
+    forward([(2 * CB, 3 * CB)])
+    stats(y_me, "all")
     got("xr_t", "xl_ot", "xl_vt", "xr_vot")
     sent("xr_t", "xl_t", "pair_t", "xl_ot", "xr_vt", "xl_vt", "xr_vot")
     loads["tmod"].wait()
@@ -410,9 +409,6 @@
     copy("hor", g.at[0, 1, Q_A], rqo.at[0], right)
     copy("hol", g.at[0, 1, Q_B], rqo.at[1], left)
     pass_on(1)
-    grad(x * 2 + ls[0], gown.at[0])
-    g[3, 0, Q_ROWS] = gown[0, Q_ROWS].astype(BF16)
-    copy("q3", g.at[3, 0, Q_ROWS], ryq.at[3], pair)
 
     loads["gen"].wait()
     loads["gate"].wait()
@@ -444,7 +440,7 @@
     teacher(0, 8)
     total = jnp.sum(jnp.sum(col[0], axis=0, keepdims=True), axis=1, keepdims=True)
     gap_s[0] = jnp.broadcast_to(total, (8, 128))
-    gap_to = (sib, on_f(yh, z + 1 - 2 * (z % 2), p), on_f(yh, 3 - z, p), across)
+    gap_to = (across, on_f(yh, z + 1 - 2 * (z % 2), p), on_f(yh, 3 - z, p), sib)
 
     def gap_step(k):
         if k:
@@ -453,6 +449,9 @@
         copy(f"gap{k}", gap_s.at[k], gap_r.at[k], gap_to[k])
 
     gap_step(0)
+    grad(x * 2 + ls[0], gown.at[0])
+    g[3, 0, Q_ROWS] = gown[0, Q_ROWS].astype(BF16)
+    copy("q3", g.at[3, 0, Q_ROWS], ryq.at[3], pair)
     got("q1", "hor")
     add(g.at[1, 1], Q_ROWS, ryq[1])
     add(g.at[1, 1], Q_A, rqo[0])

time: 136 us -> 127 us (0.934)
  Pallas kernels: 130 us -> 122 us
    pallas_call x1, Pallas kernels: 130 us -> 122 us  [per_device(): pl.pallas_call(kernel, out_shape=(jax.ShapeDtypeStruct((FB, TOK), BF16),...]
where the time goes in v5:
time: 127 us
  Pallas kernels  122 us (96%)
  local copies, waits for them, and re-layouts  4.06 us (3%)
  between operations  1.3 us (1%)
    pallas_call x1, Pallas kernels, per_device(): pl.pallas_call(kernel, out_shape=(jax.ShapeDtypeStruct((FB, TOK), BF16),...  122 us
    unnamed x7, local copies, waits for them, and re-layouts  4.06 us

profile of v5, /device:TPU:1, one launch (start us, length us, event | category | flops | bytes accessed | tf_op | source)
XLA Modules:
  0.0 127.3 jit_solution(7183250841014664051)
XLA Ops:
  1.3 121.9 %step.2 = (bf16[320,2048]{1,0:T(8,128)(2,1)}, f32[1,320]{1,0:T(1,128)}, f32[320,640]{1,0:T(8,128)}) custom-call(bf16[320,2048]{1,0:T(8,128)(2,1)} %bitcast.10, bf16[320,2048]{1,0:T(8,128)(2,1)} %bitcast.11, bf16[320,2048]{1,0:T(8,128)(2,1)} %bitcast.12, s32[1]{0:T(128)S(6)} %copy.15.step, f32[2,5120]{1,0:T(2,128)} %bitcast.16, f32[2,5120]{1,0:T(2,128)} %bitcast.17, ...), custom_call_target="tpu_custom_call" | custom-call | tf_op jit(solution)/shard_map/step/pallas_call | solution.py:508
  123.2 0.0 copy-start.1
  123.2 0.0 copy-start
  123.2 2.6 %copy.16 = bf16[2048,320]{0,1:T(8,128)(2,1)} copy(bf16[2048,320]{0,1:T(8,128)(2,1)} %bitcast.9) | data formatting | bytes 2621440
  125.8 0.0 copy-done.1
  125.8 0.6 copy.17
  126.4 0.0 copy-done
  126.4 0.9 copy.18
Async XLA Ops:
  123.2 2.6 %copy-start.1 = (f32[1,320]{1,0:T(1,128)S(1)}, f32[1,320]{1,0:T(1,128)}, u32[]{:S(2)}) copy-start(f32[1,320]{1,0:T(1,128)} %get-tuple-element.13) | copy-start | bytes 3844
  123.2 3.2 %copy-start = (f32[320,640]{1,0:T(8,128)S(1)}, f32[320,640]{1,0:T(8,128)}, u32[]{:S(2)}) copy-start(f32[320,640]{1,0:T(8,128)} %get-tuple-element.8) | copy-start | bytes 2457604

commit v6 on v5

--- a/solution.py
+++ b/solution.py
@@ -110,18 +110,18 @@
         first, n = part[which]
         return pl.ds(pl.multiple_of(first - p * FB, 64), n)
 
-    for which in ("a", "b", "c"):
+    def load_part(which):
         load("s" + which, sample.at[local(which), :], sT.at[local(which), :])
         load("n" + which, noise.at[local(which), :], nT.at[local(which), :])
-    load("fw", fw, w_ref(clip, 0))
-    load("tw", tw, w_ref(clip, 1))
-    load("fmod", fmod_in, fmod)
-    load("tmod", tmod_in, tmod)
-    load("gen", gen, gT)
-    load("gate", gate_in, gate)
+
+    load_part("a")
     barrier = pltpu.get_barrier_semaphore()
     for to in (up, dn, across, sib, right, left, pair):
         pl.semaphore_signal(barrier, inc=1, device_id=to, device_id_type=pl.DeviceIdType.MESH)
+    load_part("b")
+    load("fw", fw, w_ref(clip, 0))
+    load("tw", tw, w_ref(clip, 1))
+    load_part("c")
 
     frac = jnp.full((8, 128), step[0], jnp.int32).astype(F32) / 1000.0
     sigma = (5.0 * frac / (1.0 + 4.0 * frac))[0:1, 0:1]
@@ -162,6 +162,11 @@
     v_me, v_l, v_r, v_o = x * 2 + 1 - l, xl * 2 + 1 - l, xr * 2 + 1 - l, xo * 2 + 1 - l
     everyone = (clip, w_l, w_r, w_o, v_me, v_l, v_r, v_o)
 
+    load("fmod", fmod_in, fmod)
+    load("tmod", tmod_in, tmod)
+    load("gen", gen, gT)
+    load("gate", gate_in, gate)
+
     @pl.loop(0, 8)
     def _(i):
         cols = pl.ds(pl.multiple_of(i * 256, 256), 256)
@@ -222,9 +227,9 @@
         )
 
     def forward(spans, fresh=False, top=0):
-        @pl.loop(0, 8)
+        @pl.loop(0, 2)
         def _(i):
-            cols = pl.ds(pl.multiple_of(i * 256, 256), 256)
+            cols = pl.ds(pl.multiple_of(i * 1024, 1024), 1024)
             if fresh:
                 acc[top : top + FB, cols] = product(top, spans, cols)
             else:
@@ -368,8 +373,8 @@
             g = (part_sum - sv[:, 0:1]) * (1.0 + fmod[1:2, lanes]) + sb[:, 0:1] * fmod[0:1, lanes]
             dst[:, first : first + n] = g.astype(dst.dtype)
 
-    P_ROWS, P_A, P_B = slice(0, 192), slice(0, 96), slice(96, 192)
-    Q_ROWS, Q_A, Q_B = slice(192, 320), slice(192, 256), slice(256, 320)
+    P_ROWS, P_A, P_B = slice(0, 176), slice(0, 96), slice(96, 176)
+    Q_ROWS, Q_A, Q_B = slice(176, 320), slice(176, 240), slice(240, 320)
     ls = (1 - l, l)
 
     def add(dst, rows, *terms):
@@ -378,7 +383,7 @@
     def opposite(j):
         grad(xo * 2 + ls[j], g.at[0, j])
         copy(f"or{j}", g.at[0, j, P_A], rpo.at[0, j], right)
-        copy(f"ol{j}", g.at[0, j, P_B], rpo.at[1, j], left)
+        copy(f"ol{j}", g.at[0, j, P_B], rpo.at[1, j, 0:80], left)
 
     def next_one(j):
         grad(xr * 2 + ls[j], g.at[1, j])
@@ -395,7 +400,7 @@
         add(g.at[1, j], P_A, rpo[0, j])
         copy(f"sr{j}", g.at[1, j, P_A], rpn.at[0, j, P_A], right)
         got(f"ol{j}")
-        add(g.at[2, j], P_B, rpo[1, j])
+        add(g.at[2, j], P_B, rpo[1, j, 0:80])
         copy(f"sl{j}", g.at[2, j, P_B], rpn.at[1, j, P_B], left)
 
     opposite(0)
@@ -406,18 +411,19 @@
     next_one(1)
     got("q0")
     add(g.at[0, 1], Q_ROWS, ryq[0])
-    copy("hor", g.at[0, 1, Q_A], rqo.at[0], right)
+    copy("hor", g.at[0, 1, Q_A], rqo.at[0, 0:64], right)
     copy("hol", g.at[0, 1, Q_B], rqo.at[1], left)
     pass_on(1)
 
     loads["gen"].wait()
     loads["gate"].wait()
 
-    def teacher(first, last):
-        @pl.loop(first, last)
+    def teacher():
+        forward([(5 * CB, 3 * CB)], False, FB)
+
+        @pl.loop(0, 8)
         def _(i):
             cols = pl.ds(pl.multiple_of(i * 256, 256), 256)
-            acc[FB:CB, cols] += product(FB, [(5 * CB, 3 * CB)], cols)
             m, r = mr[0:1, cols], mr[1:2, cols]
             for k in range(0, FB, 64):
                 rows, more = slice(k, k + 64), slice(FB + k, FB + k + 64)
@@ -437,7 +443,7 @@
                 col[0, rows, :] += away[:, :128] + away[:, 128:]
                 col[1, rows, :] += pushed[:, :128] + pushed[:, 128:]
 
-    teacher(0, 8)
+    teacher()
     total = jnp.sum(jnp.sum(col[0], axis=0, keepdims=True), axis=1, keepdims=True)
     gap_s[0] = jnp.broadcast_to(total, (8, 128))
     gap_to = (across, on_f(yh, z + 1 - 2 * (z % 2), p), on_f(yh, 3 - z, p), sib)
@@ -454,7 +460,7 @@
     copy("q3", g.at[3, 0, Q_ROWS], ryq.at[3], pair)
     got("q1", "hor")
     add(g.at[1, 1], Q_ROWS, ryq[1])
-    add(g.at[1, 1], Q_A, rqo[0])
+    add(g.at[1, 1], Q_A, rqo[0, 0:64])
     copy("hr", g.at[1, 1, Q_ROWS], rqn.at[0], right)
     gap_step(1)
     got("q2", "hol")
@@ -498,6 +504,23 @@
     sent(*table)
     out_bc.wait()
     out_fg.wait()
+
+
+def hand_over(cot, gate_grad, grad, cot_out, gate_grad_out, grad_out, a, b, c, in_sems, out_sems):
+    pieces = [(gate_grad, b, gate_grad_out)]
+    for k in range(0, FB, 160):
+        rows = pl.ds(k, 160)
+        pieces.append((cot.at[rows], a.at[rows], cot_out.at[rows]))
+        pieces.append((grad.at[rows], c.at[rows], grad_out.at[rows]))
+    first = [pltpu.make_async_copy(x, y, in_sems.at[i]) for i, (x, y, _) in enumerate(pieces)]
+    second = [pltpu.make_async_copy(y, z, out_sems.at[i]) for i, (_, y, z) in enumerate(pieces)]
+    for one in first:
+        one.start()
+    for one, two in zip(first, second):
+        one.wait()
+        two.start()
+    for two in second:
+        two.wait()
 
 
 def per_device(
@@ -540,11 +563,11 @@
             pltpu.VMEM((4, 2, FB, CB), BF16),
             pltpu.VMEM((2, FB, CB), F32),
             pltpu.VMEM((2, 2, 96, CB), BF16),
-            pltpu.VMEM((2, 2, 192, CB), BF16),
-            pltpu.VMEM((4, 128, CB), BF16),
-            pltpu.VMEM((2, 64, CB), BF16),
-            pltpu.VMEM((2, 128, CB), BF16),
-            pltpu.VMEM((192, CB), BF16),
+            pltpu.VMEM((2, 2, 176, CB), BF16),
+            pltpu.VMEM((4, 144, CB), BF16),
+            pltpu.VMEM((2, 80, CB), BF16),
+            pltpu.VMEM((2, 144, CB), BF16),
+            pltpu.VMEM((176, CB), BF16),
             pltpu.VMEM((2, TOK), F32),
             pltpu.VMEM((2, TOK), F32),
             pltpu.VMEM((4, 8, 128), F32),
@@ -562,6 +585,25 @@
         teacher_mod.reshape(2, CLIPS * CB), fake_mod.reshape(2, CLIPS * CB),
         teacher_weight.T, fake_weight.T, gen_gate,
     )
+    cot, gate_grad, grad = pl.pallas_call(
+        hand_over,
+        out_shape=(
+            jax.ShapeDtypeStruct((FB, TOK), BF16),
+            jax.ShapeDtypeStruct((1, FB), F32),
+            jax.ShapeDtypeStruct((FB, CB), F32),
+        ),
+        in_specs=[hbm] * 3,
+        out_specs=(hbm,) * 3,
+        scratch_shapes=[
+            pltpu.VMEM((FB, TOK), BF16),
+            pltpu.VMEM((1, FB), F32),
+            pltpu.VMEM((FB, CB), F32),
+            pltpu.SemaphoreType.DMA((5,)),
+            pltpu.SemaphoreType.DMA((5,)),
+        ],
+        compiler_params=pltpu.CompilerParams(vmem_limit_bytes=60 << 20),
+        name="hand_over",
+    )(cot, gate_grad, grad)
     return cot.T, gate_grad, grad.T
 
 

time: 127 us -> 123 us (0.969)
  local copies, waits for them, and re-layouts: 4.06 us -> 0 us
    unnamed x7 -> x0, local copies, waits for them, and re-layouts: 4.06 us -> none
    pallas_call x1, Pallas kernels: 122 us -> 119 us  [per_device(): pl.pallas_call(kernel, out_shape=(jax.ShapeDtypeStruct((FB, TOK), BF16),...]
    pallas_call x0 -> x1, Pallas kernels: none -> 2.5 us  [per_device(): pl.pallas_call(hand_over, out_shape=(jax.ShapeDtypeStruct((FB, TOK), BF16...]
where the time goes in v6:
time: 123 us
  Pallas kernels  122 us (99%)
  between operations  1.45 us (1%)
    pallas_call x1, Pallas kernels, per_device(): pl.pallas_call(kernel, out_shape=(jax.ShapeDtypeStruct((FB, TOK), BF16),...  119 us
    pallas_call x1, Pallas kernels, per_device(): pl.pallas_call(hand_over, out_shape=(jax.ShapeDtypeStruct((FB, TOK), BF16...  2.5 us

profile of v6, /device:TPU:1, one launch (start us, length us, event | category | flops | bytes accessed | tf_op | source)
XLA Modules:
  0.0 123.0 jit_solution(8558916550066411934)
XLA Ops:
  1.3 119.0 %step.2 = (bf16[320,2048]{1,0:T(8,128)(2,1)}, f32[1,320]{1,0:T(1,128)}, f32[320,640]{1,0:T(8,128)}) custom-call(bf16[320,2048]{1,0:T(8,128)(2,1)} %bitcast.9, bf16[320,2048]{1,0:T(8,128)(2,1)} %bitcast.10, bf16[320,2048]{1,0:T(8,128)(2,1)} %bitcast.11, s32[1]{0:T(128)S(6)} %copy.12.step, f32[2,5120]{1,0:T(2,128)} %bitcast.14, f32[2,5120]{1,0:T(2,128)} %bitcast.15, ...), custom_call_target="tpu_custom_call" | custom-call | tf_op jit(solution)/shard_map/step/pallas_call | solution.py:531
  120.3 2.5 %hand_over.1 = (bf16[320,2048]{1,0:T(8,128)(2,1)}, f32[1,320]{1,0:T(1,128)}, f32[320,640]{1,0:T(8,128)}) custom-call(bf16[320,2048]{1,0:T(8,128)(2,1)} %get-tuple-element.9.cot, f32[1,320]{1,0:T(1,128)} %get-tuple-element.10.gate_grad, f32[320,640]{1,0:T(8,128)} %get-tuple-element.11.grad), custom_call_target="tpu_custom_call" | custom-call | tf_op jit(solution)/shard_map/hand_over/pallas_call | solution.py:588

commit v7 on v6

--- a/solution.py
+++ b/solution.py
@@ -27,7 +27,7 @@
 
 def kernel(
     sample, noise, gen, step, tmod_in, fmod_in, tw, fw, gate_in,
-    bc_out, gg_out, fg_out,
+    bc_out, gc_out, gg_out, fg_out,
     at, wt, acc, sT, nT, gT, vv, bt, st1, st2, piv, mr, cs, bw, sv, sb, col,
     tmod, fmod, gate, g, gown, rpo, rpn, ryq, rqo, rqn, rpy, stat_s, stat_r, gap_s, gap_r,
     send_sems, recv_sems, loc_sems,
@@ -444,6 +444,8 @@
                 col[1, rows, :] += pushed[:, :128] + pushed[:, 128:]
 
     teacher()
+    out_bc = pltpu.make_async_copy(acc.at[FB:CB], bc_out, loc_sems.at[13])
+    out_bc.start()
     total = jnp.sum(jnp.sum(col[0], axis=0, keepdims=True), axis=1, keepdims=True)
     gap_s[0] = jnp.broadcast_to(total, (8, 128))
     gap_to = (across, on_f(yh, z + 1 - 2 * (z % 2), p), on_f(yh, 3 - z, p), sib)
@@ -485,13 +487,8 @@
     gg_col = jnp.sum(col[1], axis=1, keepdims=True) * weight * (1.0 / math.sqrt(TOK))
     gg_out[...] = jnp.sum(same * gg_col, axis=0, keepdims=True)
 
-    @pl.loop(0, 8)
-    def _(i):
-        rows = pl.ds(pl.multiple_of(i * 256, 256), 256)
-        vv[:, rows] = (col[0, :, 0:1] * acc[FB:CB, rows]).astype(BF16)
-
-    out_bc = pltpu.make_async_copy(vv, bc_out, loc_sems.at[13])
-    out_bc.start()
+    out_gc = pltpu.make_async_copy(col.at[0], gc_out, loc_sems.at[12])
+    out_gc.start()
 
     got("rr1", "sr1", "rl1", "sl1")
     add(gown.at[1], P_ROWS, rpn[0, 1], rpn[1, 1])
@@ -503,22 +500,32 @@
     out_fg.start()
     sent(*table)
     out_bc.wait()
+    out_gc.wait()
     out_fg.wait()
 
 
-def hand_over(cot, gate_grad, grad, cot_out, gate_grad_out, grad_out, a, b, c, in_sems, out_sems):
-    pieces = [(gate_grad, b, gate_grad_out)]
-    for k in range(0, FB, 160):
-        rows = pl.ds(k, 160)
-        pieces.append((cot.at[rows], a.at[rows], cot_out.at[rows]))
-        pieces.append((grad.at[rows], c.at[rows], grad_out.at[rows]))
+def hand_over(
+    diff, gate, gate_grad, grad, cot_out, gate_grad_out, grad_out, a, g, b, c, d, in_sems, out_sems
+):
+    pieces = [(gate, g, None), (gate_grad, b, gate_grad_out)]
+    for k in range(0, FB, 80):
+        rows = pl.ds(k, 80)
+        pieces.append((diff.at[rows], a.at[rows], (d.at[rows], cot_out.at[rows], k)))
+    pieces.append((grad, c, grad_out))
     first = [pltpu.make_async_copy(x, y, in_sems.at[i]) for i, (x, y, _) in enumerate(pieces)]
-    second = [pltpu.make_async_copy(y, z, out_sems.at[i]) for i, (_, y, z) in enumerate(pieces)]
     for one in first:
         one.start()
-    for one, two in zip(first, second):
-        one.wait()
-        two.start()
+    second = []
+    for i, (_, y, z) in enumerate(pieces):
+        first[i].wait()
+        if z is None:
+            continue
+        if isinstance(z, tuple):
+            y, z, k = z
+            for r in range(k, k + 80, 16):
+                d[r : r + 16, :] = (g[r : r + 16, 0:1] * a[r : r + 16, :]).astype(BF16)
+        second.append(pltpu.make_async_copy(y, z, out_sems.at[i]))
+        second[-1].start()
     for two in second:
         two.wait()
 
@@ -528,17 +535,18 @@
 ):
     hbm = pl.BlockSpec(memory_space=pl.ANY)
     vmem = pl.BlockSpec(memory_space=pltpu.VMEM)
-    cot, gate_grad, grad = pl.pallas_call(
+    diff, gate, gate_grad, grad = pl.pallas_call(
         kernel,
         out_shape=(
-            jax.ShapeDtypeStruct((FB, TOK), BF16),
+            jax.ShapeDtypeStruct((FB, TOK), F32),
+            jax.ShapeDtypeStruct((FB, 128), F32),
             jax.ShapeDtypeStruct((1, FB), F32),
             jax.ShapeDtypeStruct((FB, CB), F32),
         ),
         in_specs=[
             hbm, hbm, hbm, pl.BlockSpec(memory_space=pltpu.SMEM), hbm, hbm, hbm, hbm, hbm,
         ],
-        out_specs=(hbm, vmem, hbm),
+        out_specs=(hbm, hbm, vmem, hbm),
         scratch_shapes=[
             pltpu.VMEM((CLIPS * CB, TOK), BF16),
             pltpu.VMEM((CB, CLIPS * CB), BF16),
@@ -592,18 +600,20 @@
             jax.ShapeDtypeStruct((1, FB), F32),
             jax.ShapeDtypeStruct((FB, CB), F32),
         ),
-        in_specs=[hbm] * 3,
+        in_specs=[hbm] * 4,
         out_specs=(hbm,) * 3,
         scratch_shapes=[
-            pltpu.VMEM((FB, TOK), BF16),
+            pltpu.VMEM((FB, TOK), F32),
+            pltpu.VMEM((FB, 128), F32),
             pltpu.VMEM((1, FB), F32),
             pltpu.VMEM((FB, CB), F32),
-            pltpu.SemaphoreType.DMA((5,)),
-            pltpu.SemaphoreType.DMA((5,)),
+            pltpu.VMEM((FB, TOK), BF16),
+            pltpu.SemaphoreType.DMA((7,)),
+            pltpu.SemaphoreType.DMA((7,)),
         ],
         compiler_params=pltpu.CompilerParams(vmem_limit_bytes=60 << 20),
         name="hand_over",
-    )(cot, gate_grad, grad)
+    )(diff, gate, gate_grad, grad)
     return cot.T, gate_grad, grad.T
 
 

time: 123 us -> 123 us (level)
  no operation moved by 1% of the time
where the time goes in v7:
time: 123 us
  Pallas kernels  121 us (98%)
  between operations  1.45 us (1%)
    pallas_call x1, Pallas kernels, per_device(): pl.pallas_call(kernel, out_shape=(jax.ShapeDtypeStruct((FB, TOK), F32), j...  118 us
    pallas_call x1, Pallas kernels, per_device(): pl.pallas_call(hand_over, out_shape=(jax.ShapeDtypeStruct((FB, TOK), BF16...  3.05 us

profile of v7, /device:TPU:1, one launch (start us, length us, event | category | flops | bytes accessed | tf_op | source)
XLA Modules:
  0.0 122.7 jit_solution(8954229103399797588)
XLA Ops:
  1.3 118.2 %step.2 = (f32[320,2048]{1,0:T(8,128)}, f32[320,128]{1,0:T(8,128)}, f32[1,320]{1,0:T(1,128)}, f32[320,640]{1,0:T(8,128)}) custom-call(bf16[320,2048]{1,0:T(8,128)(2,1)} %bitcast.9, bf16[320,2048]{1,0:T(8,128)(2,1)} %bitcast.10, bf16[320,2048]{1,0:T(8,128)(2,1)} %bitcast.11, s32[1]{0:T(128)S(6)} %copy.12.step, f32[2,5120]{1,0:T(2,128)} %bitcast.14, ...), custom_call_target="tpu_custom_call" | custom-call | tf_op jit(solution)/shard_map/step/pallas_call | solution.py:538
  119.5 3.0 %hand_over.1 = (bf16[320,2048]{1,0:T(8,128)(2,1)}, f32[1,320]{1,0:T(1,128)}, f32[320,640]{1,0:T(8,128)}) custom-call(f32[320,2048]{1,0:T(8,128)} %get-tuple-element.10.diff, f32[320,128]{1,0:T(8,128)} %get-tuple-element.11.gate, f32[1,320]{1,0:T(1,128)} %get-tuple-element.12.gate_grad, f32[320,640]{1,0:T(8,128)} %get-tuple-element.13.grad), custom_call_target="tpu_custom_call" | custom-call | tf_op jit(solution)/shard_map/hand_over/pallas_call | solution.py:596

commit v8 on v7

--- a/solution.py
+++ b/solution.py
@@ -364,9 +364,9 @@
     sv[...] = jnp.broadcast_to(jnp.sum(sv[...], axis=1, keepdims=True), sv.shape)
     sb[...] = jnp.broadcast_to(jnp.sum(sb[...], axis=1, keepdims=True), sb.shape)
 
-    def grad(block, dst):
+    def grad(block, dst, pieces=((0, 256), (256, 256), (512, 128))):
         held = slot(block) * CB
-        for first, n in ((0, 256), (256, 256), (512, 128)):
+        for first, n in pieces:
             lanes = pl.ds(pl.multiple_of(block * CB + first, 128), n)
             rows = pl.ds(pl.multiple_of(held + first, 128), n)
             part_sum = lax.dot_general(vv[...], at[rows, :], NT, preferred_element_type=F32)
@@ -396,14 +396,18 @@
             copy("q2", g.at[2, 0, Q_ROWS], ryq.at[2], pair)
 
     def pass_on(j):
-        got(f"or{j}")
+        got(*(("or00", "or01") if j == 0 else ("or1",)))
         add(g.at[1, j], P_A, rpo[0, j])
         copy(f"sr{j}", g.at[1, j, P_A], rpn.at[0, j, P_A], right)
-        got(f"ol{j}")
+        got(*(("ol00", "ol01") if j == 0 else ("ol1",)))
         add(g.at[2, j], P_B, rpo[1, j, 0:80])
         copy(f"sl{j}", g.at[2, j, P_B], rpn.at[1, j, P_B], left)
 
-    opposite(0)
+    for k, pieces in enumerate((((0, 256),), ((256, 256), (512, 128)))):
+        grad(xo * 2 + ls[0], g.at[0, 0], pieces)
+        lanes = slice(k * 256, CB if k else 256)
+        copy(f"or0{k}", g.at[0, 0, P_A, lanes], rpo.at[0, 0, :, lanes], right)
+        copy(f"ol0{k}", g.at[0, 0, P_B, lanes], rpo.at[1, 0, 0:80, lanes], left)
     copy("q0", g.at[0, 0, Q_ROWS], ryq.at[0], pair)
     opposite(1)
     next_one(0)

time: 123 us -> 123 us (level)
  no operation moved by 1% of the time
where the time goes in v8:
time: 123 us
  Pallas kernels  121 us (98%)
  between operations  1.45 us (1%)
    pallas_call x1, Pallas kernels, per_device(): pl.pallas_call(kernel, out_shape=(jax.ShapeDtypeStruct((FB, TOK), F32), j...  118 us
    pallas_call x1, Pallas kernels, per_device(): pl.pallas_call(hand_over, out_shape=(jax.ShapeDtypeStruct((FB, TOK), BF16...  3.05 us

profile of v8, /device:TPU:1, one launch (start us, length us, event | category | flops | bytes accessed | tf_op | source)
XLA Modules:
  0.0 122.6 jit_solution(1130813090873635659)
XLA Ops:
  1.3 118.1 %step.2 = (f32[320,2048]{1,0:T(8,128)}, f32[320,128]{1,0:T(8,128)}, f32[1,320]{1,0:T(1,128)}, f32[320,640]{1,0:T(8,128)}) custom-call(bf16[320,2048]{1,0:T(8,128)(2,1)} %bitcast.9, bf16[320,2048]{1,0:T(8,128)(2,1)} %bitcast.10, bf16[320,2048]{1,0:T(8,128)(2,1)} %bitcast.11, s32[1]{0:T(128)S(6)} %copy.12.step, f32[2,5120]{1,0:T(2,128)} %bitcast.14, ...), custom_call_target="tpu_custom_call" | custom-call | tf_op jit(solution)/shard_map/step/pallas_call | solution.py:542
  119.4 3.0 %hand_over.1 = (bf16[320,2048]{1,0:T(8,128)(2,1)}, f32[1,320]{1,0:T(1,128)}, f32[320,640]{1,0:T(8,128)}) custom-call(f32[320,2048]{1,0:T(8,128)} %get-tuple-element.10.diff, f32[320,128]{1,0:T(8,128)} %get-tuple-element.11.gate, f32[1,320]{1,0:T(1,128)} %get-tuple-element.12.gate_grad, f32[320,640]{1,0:T(8,128)} %get-tuple-element.13.grad), custom_call_target="tpu_custom_call" | custom-call | tf_op jit(solution)/shard_map/hand_over/pallas_call | solution.py:600
